TPU v7x, 32 devices: a whole 2x2x4 slice. The times are simulated.
32 devices in a mesh: section: 4 (over y, x), seq: 8 (over z, core), dp: 1.
Axes of the slice: x: 2, y: 2, z: 4, core: 2. Of those that a mesh axis runs over, the one named last changes fastest.
Arguments:
- roles: int32 [4], replicated, may hold values from 0 to 3, each once
- block_ids: int32 [2, 1, 1536], P(None, 'dp'), may hold values from 0 to 15, never falling along the last dimension, each value on 1 to 384 neighbouring positions
- latent: bfloat16 [1, 1536, 2560], P('dp', 'seq'), may hold values from -6 to 6
- pending: bfloat16 [1, 1536, 2560], P('dp', 'seq'), may hold values from -6 to 6
- context: float32 [1, 2560], P('dp'), may hold values from -6 to 6
- w_qkv: bfloat16 [3, 2560, 6144], P(None, None, 'seq'), may hold values from -3.3796842 to 3.3796842
- w_out: bfloat16 [3, 2048, 2560], P(None, 'seq'), may hold values from -0.125 to 0.125
- stored_attn: bfloat16 [1, 1536, 2048], P('dp', None, 'seq'), may hold values from -1.5 to 1.5
Outputs:
- block_out: bfloat16 [4, 1, 1536, 2560], P('section', 'dp', 'seq')
- dmd_grad: float32 [1, 1536, 2560], P('dp', 'seq')
- grad_out: float32 [2048, 2560], P('seq')
Inputs may be any that keep to these rules, and one draw needn't show every extreme that they name: `roles`: each section has a different role: 0 generator, 1 teacher with context, 2 teacher without context, 3 fake-score model. `block_ids`: never falling along frames, starting at 0; each block has 1 to 384 frames, and one block of each row has exactly 384.
All inputs are finite; a program needn't handle non-finite values.
Results may differ from a plain program's by a relative error of at most 0.0083.
Values may be sent and summed in bfloat16 or wider, within the bound.
A program may use at most 128 MiB of HBM per device.

v0:
```python
import jax
import jax.numpy as jnp
from jax import lax
from jax.sharding import PartitionSpec as P

HEAD_DIM = 128


GUIDE = 3.0
EPSILON = 1e-06
NEGATIVE = -1e30


def attend(qkv_rows, frame_ids):
    length = qkv_rows.shape[0]
    heads_here = qkv_rows.shape[1] // (3 * HEAD_DIM)
    split = qkv_rows.reshape(length, heads_here, 3, HEAD_DIM).transpose(1, 2, 0, 3)
    block_size = min(512, length)
    block_count = length // block_size
    scale = HEAD_DIM ** (-0.5)

    def per_head(triple):
        queries = triple[0]
        keys_all = triple[1]
        values = triple[2]

        def per_block(args):
            query_rows, query_ids = args
            scores = (
                lax.dot_general(
                    query_rows,
                    keys_all,
                    (((1,), (1,)), ((), ())),
                    preferred_element_type=jnp.float32,
                )
                * scale
            )
            visible = frame_ids[None, :] <= query_ids[:, None]
            scores = jnp.where(visible, scores, NEGATIVE)
            highest = jnp.max(scores, axis=1, keepdims=True)
            expon = jnp.where(visible, jnp.exp(scores - highest), 0.0)
            probs = (expon / jnp.sum(expon, axis=1, keepdims=True)).astype(jnp.bfloat16)
            return jnp.dot(probs, values, preferred_element_type=jnp.float32).astype(jnp.bfloat16)

        blocks = lax.map(
            per_block,
            (
                queries.reshape(block_count, block_size, HEAD_DIM),
                frame_ids.reshape(block_count, block_size),
            ),
        )
        return blocks.reshape(length, HEAD_DIM)

    heads_out = lax.map(per_head, split)
    return heads_out.transpose(1, 0, 2).reshape(length, heads_here * HEAD_DIM)


def per_device(roles, block_ids, latent, pending, context, w_qkv, w_out, stored_attn):
    section = lax.axis_index("section")
    places = jnp.arange(4, dtype=jnp.int32)
    weight_table = jnp.array([0.0, -GUIDE, GUIDE - 1.0, 1.0], jnp.float32)
    section_role = jnp.sum(jnp.where(places == section, roles, 0))
    model_index = jnp.sum(jnp.where(places == section_role, jnp.array([0, 1, 1, 2], jnp.int32), 0))
    score_weight = jnp.sum(jnp.where(places == section_role, weight_table, 0.0))
    w_in = lax.dynamic_index_in_dim(w_qkv, model_index, 0, keepdims=False)
    w_proj = lax.dynamic_index_in_dim(w_out, model_index, 0, keepdims=False)
    is_generator = section_role == 0
    with_context = jnp.logical_or(section_role == 1, section_role == 3).astype(jnp.float32)
    width = latent.shape[2]
    scored = pending[0].astype(jnp.float32) + with_context * context[0][None, :]
    source = jnp.where(is_generator, latent[0].astype(jnp.float32), scored)
    normed = (
        source * lax.rsqrt(jnp.mean(source * source, axis=1, keepdims=True) + EPSILON)
    ).astype(jnp.bfloat16)
    qkv_rows = jnp.dot(
        lax.all_gather(normed, "seq", axis=0, tiled=True), w_in, preferred_element_type=jnp.float32
    ).astype(jnp.bfloat16)
    frame_ids = jnp.where(is_generator, block_ids[0, 0], block_ids[1, 0])
    attn = attend(qkv_rows, frame_ids)
    local_attn = lax.all_to_all(attn, "seq", split_axis=0, concat_axis=1, tiled=True)
    branch = jnp.dot(
        local_attn,
        lax.all_gather(w_proj, "seq", axis=0, tiled=True),
        preferred_element_type=jnp.float32,
    )
    outputs = [(source + branch).astype(jnp.bfloat16)]
    branches = [branch]
    block_out = jnp.stack(outputs)[None]
    branch_all = jnp.stack(branches)
    gradient = lax.psum(score_weight * branch_all, "section")
    grad_bf = gradient.astype(jnp.bfloat16)
    column_width = width // lax.axis_size("section")
    first_column = section * column_width
    grad_columns = lax.dynamic_slice_in_dim(grad_bf, first_column, column_width, 2)
    inner_here = stored_attn.shape[2]
    local_grad = jnp.einsum(
        "bri,brc->ic",
        stored_attn,
        lax.all_gather(grad_columns, "seq", axis=1, tiled=True),
        preferred_element_type=jnp.float32,
    )
    placed = lax.dynamic_update_slice_in_dim(
        jnp.zeros((inner_here, width), jnp.float32), local_grad, first_column, 1
    )
    grad_out = lax.psum(placed, ("section", "dp"))
    return (block_out, gradient, grad_out)


def solution(mesh):
    placed = (
        P(),
        P(None, "dp", None),
        P("dp", "seq", None),
        P("dp", "seq", None),
        P("dp", None),
        P(None, None, "seq"),
        P(None, "seq", None),
        P("dp", None, "seq"),
    )
    return jax.shard_map(
        per_device,
        mesh=mesh,
        in_specs=placed,
        out_specs=(P("section", "dp", "seq", None), P("dp", "seq", None), P("seq", None)),
        check_vma=False,
    )
```

profile of v0, /device:TPU:0, one launch (start us, length us, event | category | flops | bytes accessed | tf_op | source)
XLA Modules:
  0.0 412.1 jit_solution(16460357311089108236)
XLA Ops:
  11.4 2.0 multiply_reduce_fusion
  18.0 2.5 constant_dynamic-slice_fusion.2
  20.5 74.8 %all-gather.5.cloned.1.call-done = bf16[1536,2560]{1,0:T(8,128)(2,1)} async-done(((bf16[192,2560]{1,0:T(8,128)(2,1)}), bf16[1536,2560]{1,0:T(8,128)(2,1)}) %all-gather.5.cloned.1.call-update) | async-done | bytes 7864336 | tf_op jit(solution)/shard_map/all_gather | solution.py:76
  95.3 10.9 %fusion.14 = bf16[1536,768]{0,1:T(8,128)(2,1)} fusion(bf16[1536,2560]{1,0:T(8,128)(2,1)} %all-gather.5.cloned.1.call-done, bf16[3,2560,768]{2,1,0:T(8,128)(2,1)} %param.19, s32[]{:T(128)S(6)} %select_n.52), kind=kOutput, calls=%fused_computation.23 | convolution fusion | flops 6040977408 | bytes 14155780 | tf_op jit(solution)/shard_map/dot_general | solution.py:75
  106.2 3.1 copy.15
  109.3 30.4 %while.23 = (s32[]{:T(128)}, bf16[2,1536,128]{2,1,0:T(8,128)(2,1)}, bf16[2,3,1536,128]{3,2,1,0:T(8,128)(2,1)S(1)}, s32[1536]{0:T(1024)S(1)}, s32[3,512]{1,0:T(4,...) while((s32[]{:T(128)}, bf16[2,1536,128]{2,1,0:T(8,128)(2,1)}, ...), condition=%wide.wide.region_8.9_spmd, body=%wide.wide.region_3.8_spmd.sunk | while | flops 412941312 | bytes 13670726 | solution.py:54
  110.3 12.4 %while.24 = (s32[]{:T(128)}, bf16[3,512,128]{2,1,0:T(8,128)(2,1)}, s32[1536]{0:T(1024)S(1)}, s32[3,512]{1,0:T(4,128)S(1)}, bf16[3,512,128]{2,1,0:T(8,128)(2,1)},...) while((s32[]{:T(128)}, bf16[3,512,128]{2,1,0:T(8,128)(2,1)}, s32[1536]{0:T(1024)S(1)}, ...), condition=%wide.region_7.7_spmd, body=%wide.region_4.6_spmd.sunk | while | flops 412941312 | bytes 10524777 | solution.py:45
  110.3 1.8 fusion.44
  112.9 1.6 fusion.46
  114.5 1.8 fusion.44
  117.0 1.6 fusion.46
  118.6 1.8 fusion.44
  121.2 1.6 fusion.46
  122.8 1.8 bitcast_dynamic-update-slice_fusion.3
  125.5 12.4 %while.24 = (s32[]{:T(128)}, bf16[3,512,128]{2,1,0:T(8,128)(2,1)}, s32[1536]{0:T(1024)S(1)}, s32[3,512]{1,0:T(4,128)S(1)}, bf16[3,512,128]{2,1,0:T(8,128)(2,1)},...) while((s32[]{:T(128)}, bf16[3,512,128]{2,1,0:T(8,128)(2,1)}, s32[1536]{0:T(1024)S(1)}, ...), condition=%wide.region_7.7_spmd, body=%wide.region_4.6_spmd.sunk | while | flops 412941312 | bytes 10524777 | solution.py:45
  125.5 1.8 fusion.44
  129.6 1.8 fusion.44
  132.2 1.6 fusion.46
  133.8 1.8 fusion.44
  136.4 1.6 fusion.46
  137.9 1.8 bitcast_dynamic-update-slice_fusion.3
  139.7 6.7 %copy.16 = bf16[1536,2,128]{2,1,0:T(2,128)(2,1)S(1)} copy(bf16[1536,2,128]{2,0,1:T(8,128)(2,1)} %bitcast.89) | data formatting | bytes 1572864 | tf_op jit(solution)/shard_map/transpose | solution.py:55
  147.9 3.5 all-to-all-start
  152.9 38.8 %all-to-all-done = bf16[8,192,256]{2,1,0:T(8,128)(2,1)S(1)} async-done(((bf16[8,192,256]{2,1,0:T(8,128)(2,1)}), bf16[8,192,256]{2,1,0:T(8,128)(2,1)S(1)}, u32[]{:S(2)}, u32[]{:S(2)}) %all-to-all-start) | async-done | bytes 786464 | tf_op jit(solution)/shard_map/all_to_all | solution.py:80
  192.7 19.5 %all-gather.9.cloned.1.call-done = bf16[1,2048,2560]{2,1,0:T(8,128)(2,1)} async-done(((bf16[1,256,2560]{2,1,0:T(8,128)(2,1)}), bf16[1,2048,2560]{2,1,0:T(8,128)(2,1)}) %all-gather.9.cloned.1.call-update) | async-done | bytes 10485776 | tf_op jit(solution)/shard_map/all_gather | solution.py:83
  212.2 8.7 %multiply_bitcast_fusion = (f32[1,192,2560]{2,1,0:T(8,128)}, bf16[1,1,192,2560]{3,2,1,0:T(8,128)(2,1)}) fusion(f32[]{:T(128)} %fusion.28, f32[2560]{0:T(1024)S(1)} %copy-done.9, bf16[1,192,2560]{2,1,0:T(8,128)(2,1)S(1)} %copy-done.3, bf16[1,192,2560]{2,1,0:T(8,128)(2,1)S(1)} %copy-done.5, pred[]{:T(512)S(6)} %eq.25, bf16[192,2048]{1,0:T(8,128)(2,1)} %bitcast.90, ...), kind=kOutput, calls=%fused_computation.28 | convolution fusion | flops 2016706560 | bytes 16197637 | tf_op jit(solution)/shard_map/dot_general | solution.py:81
  221.0 65.8 %all-reduce.3.cloned.1.call-done = f32[1,192,2560]{2,1,0:T(8,128)} async-done(((f32[1,192,2560]{2,1,0:T(8,128)}), f32[1,192,2560]{2,1,0:T(8,128)}) %all-reduce.3.cloned.1.call-update) | async-done | bytes 1966096 | tf_op jit(solution)/shard_map/psum | solution.py:90
  286.7 1.8 dynamic-slice_convert_fusion
  288.6 28.3 %all-gather.7.cloned.1.call-done = bf16[1,1536,640]{2,1,0:T(8,128)(2,1)} async-done(((bf16[1,192,640]{2,1,0:T(8,128)(2,1)}), bf16[1,1536,640]{2,1,0:T(8,128)(2,1)}) %all-gather.7.cloned.1.call-update) | async-done | bytes 1966096 | tf_op jit(solution)/shard_map/all_gather | solution.py:99
  316.9 2.3 fusion.20
  322.9 78.1 %all-reduce.5.cloned.1.call-done = f32[256,2560]{1,0:T(8,128)} async-done(((f32[256,2560]{1,0:T(8,128)}), f32[256,2560]{1,0:T(8,128)}) %all-reduce.5.cloned.1.call-update) | async-done | bytes 2621456 | tf_op jit(solution)/shard_map/psum | solution.py:105
  401.0 3.1 copy.39
  (68 shorter events, 22.3 us)
Async XLA Ops:
  7.2 309.7 %copy-start = (bf16[1,1536,256]{2,1,0:T(8,128)(2,1)S(1)}, bf16[1,1536,256]{2,1,0:T(8,128)(2,1)}, u32[]{:S(2)}) copy-start(bf16[1,1536,256]{2,1,0:T(8,128)(2,1)} %param.21) | copy-start | bytes 2359300
  7.2 6.2 %copy-start.2 = (bf16[1,192,2560]{2,1,0:T(8,128)(2,1)S(1)}, bf16[1,192,2560]{2,1,0:T(8,128)(2,1)}, u32[]{:S(2)}) copy-start(bf16[1,192,2560]{2,1,0:T(8,128)(2,1)} %param.17) | copy-start | bytes 2949124
  7.2 6.2 %copy-start.4 = (bf16[1,192,2560]{2,1,0:T(8,128)(2,1)S(1)}, bf16[1,192,2560]{2,1,0:T(8,128)(2,1)}, u32[]{:S(2)}) copy-start(bf16[1,192,2560]{2,1,0:T(8,128)(2,1)} %param.16) | copy-start | bytes 2949124
  7.2 88.1 %all-gather.5.cloned.1.call-start = ((), (), s32[]{:S(2)}) async-start(), calls=%async_computation.1 | async-start | bytes 8847360 | tf_op jit(solution)/shard_map/all_gather | solution.py:76
  11.4 2.0 copy-start.8
  11.4 3.4 copy-start.12
  14.7 5.8 %copy-start.10 = (s32[2,1,1536]{2,1,0:T(1,128)S(1)}, s32[2,1,1536]{2,1,0:T(1,128)}, u32[]{:S(2)}) copy-start(s32[2,1,1536]{2,1,0:T(1,128)} %param.15) | copy-start | bytes 36868
  14.7 197.5 %all-gather.9.cloned.1.call-start = ((), (), s32[]{:S(2)}) async-start(), calls=%async_computation.5 | async-start | bytes 11796480 | tf_op jit(solution)/shard_map/all_gather | solution.py:83
  139.7 11.9 %copy-start.11 = (f32[4]{0:T(128)S(1)}, f32[4]{0:T(128)}, u32[]{:S(2)}) copy-start(f32[4]{0:T(128)} %constant.68.clone) | copy-start | bytes 52
  146.5 65.7 %copy-start.3 = (bf16[1,192,2560]{2,1,0:T(8,128)(2,1)S(1)}, bf16[1,192,2560]{2,1,0:T(8,128)(2,1)}, u32[]{:S(2)}) copy-start(bf16[1,192,2560]{2,1,0:T(8,128)(2,1)} %param.17) | copy-start | bytes 2949124
  146.5 65.7 %copy-start.5 = (bf16[1,192,2560]{2,1,0:T(8,128)(2,1)S(1)}, bf16[1,192,2560]{2,1,0:T(8,128)(2,1)}, u32[]{:S(2)}) copy-start(bf16[1,192,2560]{2,1,0:T(8,128)(2,1)} %param.16) | copy-start | bytes 2949124
  146.5 65.7 %copy-start.9 = (f32[2560]{0:T(1024)S(1)}, f32[2560]{0:T(1024)}, u32[]{:S(2)}) copy-start(f32[2560]{0:T(1024)} %copy-done.8) | copy-start | bytes 30724
  147.9 43.8 %all-to-all-start = ((bf16[8,192,256]{2,1,0:T(8,128)(2,1)}), bf16[8,192,256]{2,1,0:T(8,128)(2,1)S(1)}, u32[]{:S(2)}, u32[]{:S(2)}) async-start(bf16[8,192,256]{2,1,0:T(8,128)(2,1)} %all_to_all.14), calls=%async_computation | async-start | bytes 1572864 | tf_op jit(solution)/shard_map/all_to_all | solution.py:80
  151.4 135.3 %all-reduce.3.cloned.1.call-start = ((), (), s32[]{:S(2)}) async-start(), calls=%async_computation.2 | async-start | bytes 3932160 | tf_op jit(solution)/shard_map/psum | solution.py:90
  220.9 95.9 %all-gather.7.cloned.1.call-start = ((), (), s32[]{:S(2)}) async-start(), calls=%async_computation.3 | async-start | bytes 2211840 | tf_op jit(solution)/shard_map/all_gather | solution.py:99
  288.5 112.5 %all-reduce.5.cloned.1.call-start = ((), (), s32[]{:S(2)}) async-start(), calls=%async_computation.4 | async-start | bytes 5242880 | tf_op jit(solution)/shard_map/psum | solution.py:105
  320.2 1.1 copy-start.7
  321.4 1.5 copy-start.1
  401.0 3.1 copy-start.6
Sparse Core Ops, SparseCore 0:
  14.9 80.4 all-gather.4
  97.5 114.6 all-gather.8
  221.0 65.6 all-reduce.2
  288.8 28.0 all-gather.6
  323.0 77.9 all-reduce.4
where the time goes:
time: 413 us; the launch traced here: 412 us
  waiting for transfers between devices  305 us (74%)
  matrix products  42 us (10%)
  local copies, waits for them, and re-layouts  30.3 us (7%)
  between operations  17.8 us (4%)
  other arithmetic  12.6 us (3%)
    psum x1, waiting for transfers between devices, per_device(): grad_out = lax.psum(placed, ('section', 'dp'))  78.1 us
    all_gather x1, waiting for transfers between devices, per_device(): lax.all_gather(normed, 'seq', axis=0, tiled=True)  74.8 us
    psum x1, waiting for transfers between devices, per_device(): gradient = lax.psum(score_weight * branch_all, 'section')  65.8 us
    all_to_all x1, waiting for transfers between devices, per_device(): lax.all_to_all(attn, 'seq', split_axis=0, concat_axis=1, tiled=True)  38.8 us
    all_gather x1, waiting for transfers between devices, per_device(): lax.all_gather(grad_columns, 'seq', axis=1, tiled=True)  28.3 us
    all_gather x1, waiting for transfers between devices, per_device(): lax.all_gather(w_proj, 'seq', axis=0, tiled=True)  19.5 us
    dot_general x1, matrix products, per_device(): jnp.dot(lax.all_gather(normed, 'seq', axis=0, tiled=True), w_in, preferre...  10.9 us
    dot_general x6, matrix products, per_block(): lax.dot_general(query_rows, keys_all, (((1,), (1,)), ((), ())), preferred...  10.7 us
  transfers between devices with their start and end apart: 6, of which 6 were waited for; matrix products, arithmetic and copies ran while one was open for 14% of the time, Pallas kernels for 0%

commit v1 on v0

v1 whole, which is shorter than its diff:
```python
import functools

import jax
import jax.numpy as jnp
from jax import lax
from jax.experimental import pallas as pl
from jax.experimental.pallas import tpu as pltpu
from jax.sharding import PartitionSpec as P

HEAD_DIM = 128
GUIDE = 3.0
EPSILON = 1e-06
NEGATIVE = -1e30
SPAN_MOST = 384
LOG2E = 1.4426950408889634


def attend_kernel(ids_col, ids_row, qkv, out):
    length = qkv.shape[0]
    heads = qkv.shape[1] // (3 * HEAD_DIM)
    rows = min(256, length)
    factor = HEAD_DIM ** (-0.5) * LOG2E
    for block in range(length // rows):
        first = block * rows
        seen = min(length, first + rows + SPAN_MOST)
        hidden = ids_row[:, :seen] > ids_col[first:first + rows, :]
        for head in range(heads):
            base = head * 3 * HEAD_DIM
            query = qkv[first:first + rows, base:base + HEAD_DIM]
            keys = qkv[:seen, base + HEAD_DIM:base + 2 * HEAD_DIM]
            values = qkv[:seen, base + 2 * HEAD_DIM:base + 3 * HEAD_DIM]
            scores = lax.dot_general(
                query, keys, (((1,), (1,)), ((), ())), preferred_element_type=jnp.float32
            )
            scores = jnp.where(hidden, NEGATIVE, scores)
            highest = jnp.max(scores, axis=1, keepdims=True)
            expon = jnp.exp2((scores - highest) * factor)
            total = jnp.sum(expon, axis=1, keepdims=True)
            mixed = jnp.dot(
                expon.astype(jnp.bfloat16), values, preferred_element_type=jnp.float32
            )
            out[first:first + rows, head * HEAD_DIM:(head + 1) * HEAD_DIM] = (
                mixed / total
            ).astype(jnp.bfloat16)


def attend(qkv_rows, frame_ids):
    length, width = qkv_rows.shape
    heads = width // (3 * HEAD_DIM)
    vmem = pl.BlockSpec(memory_space=pltpu.VMEM)
    return pl.pallas_call(
        attend_kernel,
        out_shape=jax.ShapeDtypeStruct((length, heads * HEAD_DIM), jnp.bfloat16),
        in_specs=[vmem] * 3,
        out_specs=vmem,
        compiler_params=pltpu.CompilerParams(vmem_limit_bytes=48 << 20),
        cost_estimate=pl.CostEstimate(
            flops=4 * length * length * HEAD_DIM * heads,
            bytes_accessed=qkv_rows.size * 3,
            transcendentals=length * length * heads,
        ),
    )(frame_ids[:, None], frame_ids[None, :], qkv_rows)


def per_device(roles, block_ids, latent, pending, context, w_qkv, w_out, stored_attn):
    section = lax.axis_index("section")
    sections = lax.axis_size("section")
    places = jnp.arange(4, dtype=jnp.int32)
    weight_table = jnp.array([0.0, -GUIDE, GUIDE - 1.0, 1.0], jnp.float32)
    section_role = jnp.sum(jnp.where(places == section, roles, 0))
    model_index = jnp.sum(jnp.where(places == section_role, jnp.array([0, 1, 1, 2], jnp.int32), 0))
    score_weight = jnp.sum(jnp.where(places == section_role, weight_table, 0.0))
    w_in = lax.dynamic_index_in_dim(w_qkv, model_index, 0, keepdims=False)
    w_proj = lax.dynamic_index_in_dim(w_out, model_index, 0, keepdims=False)
    is_generator = section_role == 0
    with_context = jnp.logical_or(section_role == 1, section_role == 3).astype(jnp.float32)
    width = latent.shape[2]
    scored = pending[0].astype(jnp.float32) + with_context * context[0][None, :]
    source = jnp.where(is_generator, latent[0].astype(jnp.float32), scored)
    normed = (
        source * lax.rsqrt(jnp.mean(source * source, axis=1, keepdims=True) + EPSILON)
    ).astype(jnp.bfloat16)
    qkv_rows = jnp.dot(
        lax.all_gather(normed, "seq", axis=0, tiled=True), w_in, preferred_element_type=jnp.float32
    ).astype(jnp.bfloat16)
    frame_ids = jnp.where(is_generator, block_ids[0, 0], block_ids[1, 0])
    attn = attend(qkv_rows, frame_ids)
    local_attn = lax.all_to_all(attn, "seq", split_axis=0, concat_axis=1, tiled=True)
    branch = jnp.dot(
        local_attn,
        lax.all_gather(w_proj, "seq", axis=0, tiled=True),
        preferred_element_type=jnp.float32,
    )
    block_out = (source + branch).astype(jnp.bfloat16)[None, None]
    rows = branch.shape[0]
    quarter = width // sections
    terms = (score_weight * branch).astype(jnp.bfloat16)
    terms = terms.reshape(rows, sections, quarter).transpose(1, 0, 2)
    terms = lax.all_to_all(terms, "section", split_axis=0, concat_axis=0, tiled=True)
    grad_bf = jnp.sum(terms.astype(jnp.float32), axis=0).astype(jnp.bfloat16)
    gradient = lax.all_gather(grad_bf, "section", axis=1, tiled=True).astype(jnp.float32)
    grad_rows = lax.all_gather(grad_bf, "seq", axis=0, tiled=True)
    local_grad = lax.dot_general(
        stored_attn[0], grad_rows, (((0,), (0,)), ((), ())), preferred_element_type=jnp.float32
    )
    local_grad = lax.psum(local_grad, "dp").astype(jnp.bfloat16)
    grad_out = lax.all_gather(local_grad, "section", axis=1, tiled=True).astype(jnp.float32)
    return (block_out, gradient[None], grad_out)


def solution(mesh):
    placed = (
        P(),
        P(None, "dp", None),
        P("dp", "seq", None),
        P("dp", "seq", None),
        P("dp", None),
        P(None, None, "seq"),
        P(None, "seq", None),
        P("dp", None, "seq"),
    )
    return jax.shard_map(
        per_device,
        mesh=mesh,
        in_specs=placed,
        out_specs=(P("section", "dp", "seq", None), P("dp", "seq", None), P("seq", None)),
        check_vma=False,
    )
```

time: 413 us -> 308 us (0.75)
  waiting for transfers between devices: 305 us -> 202 us
  blocking collectives: 0 us -> 36.3 us
  local copies, waits for them, and re-layouts: 30.3 us -> 6.69 us
  matrix products: 42 us -> 20.7 us
  Pallas kernels: 0 us -> 8.5 us
    psum x2 -> x0, waiting for transfers between devices: 144 us -> none  [the longest x1 78.1 us: per_device(): grad_out = lax.psum(placed, ('section', 'dp'))]
    all_gather x1, waiting for transfers between devices: 19.5 us -> 50.2 us  [per_device(): lax.all_gather(w_proj, 'seq', axis=0, tiled=True)]
    dot_general x13 -> x1, matrix products: 22.5 us -> 2.99 us  [per_device(): lax.dot_general(stored_attn[0], grad_rows, (((0,), (0,)), ((), ())), pref...]
    all_gather x0 -> x1, blocking collectives: none -> 18.9 us  [per_device(): lax.all_gather(grad_bf, 'section', axis=1, tiled=True).astype(jnp.float32)]
    all_to_all x0 -> x1, blocking collectives: none -> 17.5 us  [per_device(): lax.all_to_all(terms, 'section', split_axis=0, concat_axis=0, tiled=True)]
    pallas_call x0 -> x1, Pallas kernels: none -> 8.5 us  [attend(): pl.pallas_call(attend_kernel, out_shape=jax.ShapeDtypeStruct((length, hea...]
    all_gather x1 -> x2, waiting for transfers between devices: 28.3 us -> 35.9 us  [the longest x1 24.7 us: per_device(): grad_rows = lax.all_gather(grad_bf, 'seq', axis=0, tiled=True)]
    transpose x1 -> x0, local copies, waits for them, and re-layouts: 6.72 us -> none  [attend(): return heads_out.transpose(1, 0, 2).reshape(length, heads_here * HEAD_DIM)]
  transfers between devices with their start and end apart: 6 -> 5, of which waited for: 6 -> 5; matrix products, arithmetic and copies ran while one was open for 14% -> 6% of each run, Pallas kernels for 0% -> 3%
where the time goes in v1:
time: 308 us; the launch traced here: 307 us
  waiting for transfers between devices  202 us (66%)
  blocking collectives  36.3 us (12%)
  matrix products  20.7 us (7%)
  between operations  17.8 us (6%)
  other arithmetic  11.1 us (4%)
  Pallas kernels  8.5 us (3%)
  local copies, waits for them, and re-layouts  6.69 us (2%)
  starting transfers between devices  4.02 us (1%)
    all_gather x1, waiting for transfers between devices, per_device(): lax.all_gather(normed, 'seq', axis=0, tiled=True)  73.7 us
    all_gather x1, waiting for transfers between devices, per_device(): lax.all_gather(w_proj, 'seq', axis=0, tiled=True)  50.2 us
    all_to_all x1, waiting for transfers between devices, per_device(): lax.all_to_all(attn, 'seq', split_axis=0, concat_axis=1, tiled=True)  42.4 us
    all_gather x1, waiting for transfers between devices, per_device(): grad_rows = lax.all_gather(grad_bf, 'seq', axis=0, tiled=True)  24.7 us
    all_gather x1, blocking collectives, per_device(): lax.all_gather(grad_bf, 'section', axis=1, tiled=True).astype(jnp.float32)  18.9 us
    all_to_all x1, blocking collectives, per_device(): lax.all_to_all(terms, 'section', split_axis=0, concat_axis=0, tiled=True)  17.5 us
    all_gather x1, waiting for transfers between devices, per_device(): lax.all_gather(local_grad, 'section', axis=1, tiled=True)  11.1 us
    dot_general x1, matrix products, per_device(): jnp.dot(lax.all_gather(normed, 'seq', axis=0, tiled=True), w_in, preferre...  9.74 us
  transfers between devices with their start and end apart: 5, of which 5 were waited for; matrix products, arithmetic and copies ran while one was open for 6% of the time, Pallas kernels for 3%

profile of v1, /device:TPU:0, one launch (start us, length us, event | category | flops | bytes accessed | tf_op | source)
XLA Modules:
  0.0 307.4 jit_solution(5226543448322924577)
XLA Ops:
  7.2 0.0 all-gather.6.cloned.1.call-start
  7.3 1.4 fusion.14
  10.6 0.7 multiply_reduce_fusion.1
  11.4 2.0 multiply_reduce_fusion
  13.4 1.3 multiply_convert_fusion.1
  14.7 0.0 all-gather.6.cloned.1.call-update
  14.7 0.0 all-gather.12.cloned.1.call-start
  14.8 1.3 fusion.12
  18.0 2.5 constant_dynamic-slice_fusion
  20.5 0.0 all-gather.12.cloned.1.call-update
  20.6 0.3 copy.17.ids_col
  20.9 0.7 fusion.21.ids_row
  21.6 73.7 %all-gather.6.cloned.1.call-done = bf16[1536,2560]{1,0:T(8,128)(2,1)} async-done(((bf16[192,2560]{1,0:T(8,128)(2,1)}), bf16[1536,2560]{1,0:T(8,128)(2,1)}) %all-gather.6.cloned.1.call-update) | async-done | bytes 7864336 | tf_op jit(solution)/shard_map/all_gather | solution.py:84
  95.3 9.7 %fusion.5.qkv = bf16[1536,768]{1,0:T(8,128)(2,1)S(1)} fusion(bf16[1536,2560]{1,0:T(8,128)(2,1)} %all-gather.6.cloned.1.call-done, bf16[3,2560,768]{2,1,0:T(8,128)(2,1)} %param.15, s32[]{:T(128)S(6)} %select_n.62), kind=kOutput, calls=%fused_computation.5 | convolution fusion | flops 6040977408 | bytes 14155780 | tf_op jit(solution)/shard_map/dot_general | solution.py:83
  105.1 8.5 %shard_map.121 = bf16[1536,256]{1,0:T(8,128)(2,1)} custom-call(s32[1536,1]{1,0:T(8,128)S(1)} %copy.17.ids_col, s32[1,1536]{1,0:T(1,128)S(1)} %fusion.21.ids_row, bf16[1536,768]{1,0:T(8,128)(2,1)S(1)} %fusion.5.qkv), custom_call_target="tpu_custom_call" | custom-call | flops 2415919104 | bytes 3538944 | tf_op jit(solution)/shard_map/pallas_call | solution.py:51
  113.6 3.7 %all-to-all-start = ((bf16[8,192,256]{2,1,0:T(8,128)(2,1)}), bf16[8,192,256]{2,1,0:T(8,128)(2,1)S(1)}, u32[]{:S(2)}, u32[]{:S(2)}) async-start(bf16[8,192,256]{2,1,0:T(8,128)(2,1)} %bitcast.5), calls=%async_computation | async-start | bytes 1572864 | tf_op jit(solution)/shard_map/all_to_all | solution.py:88
  117.3 0.2 all-gather.8.cloned.1.call-start
  117.5 1.2 fusion.13
  118.8 42.4 %all-to-all-done = bf16[8,192,256]{2,1,0:T(8,128)(2,1)S(1)} async-done(((bf16[8,192,256]{2,1,0:T(8,128)(2,1)}), bf16[8,192,256]{2,1,0:T(8,128)(2,1)S(1)}, u32[]{:S(2)}, u32[]{:S(2)}) %all-to-all-start) | async-done | bytes 786464 | tf_op jit(solution)/shard_map/all_to_all | solution.py:88
  161.1 1.0 copy.22
  162.1 50.2 %all-gather.12.cloned.1.call-done = bf16[1,2048,2560]{2,1,0:T(8,128)(2,1)} async-done(((bf16[1,256,2560]{2,1,0:T(8,128)(2,1)}), bf16[1,2048,2560]{2,1,0:T(8,128)(2,1)}) %all-gather.12.cloned.1.call-update) | async-done | bytes 10485776 | tf_op jit(solution)/shard_map/all_gather | solution.py:91
  212.3 8.0 %multiply_convert_fusion = (bf16[192,2560]{1,0:T(8,128)(2,1)S(1)}, bf16[1,1,192,2560]{3,2,1,0:T(8,128)(2,1)}) fusion(f32[]{:T(128)} %fusion.13, f32[2560]{0:T(1024)S(1)} %copy-done.5, bf16[1,192,2560]{2,1,0:T(8,128)(2,1)S(1)} %copy-done.1, bf16[1,192,2560]{2,1,0:T(8,128)(2,1)S(1)} %copy-done.2, pred[]{:T(512)S(6)} %eq.25, bf16[192,2048]{1,0:T(8,128)(2,1)} %bitcast.51, ...), kind=kOutput, calls=%fused_computation.8 | convolution fusion | flops 2017198080 | bytes 15214597 | tf_op jit(solution)/shard_map/dot_general | solution.py:89
  220.2 0.1 copy.24
  220.3 17.5 %all_to_all.24 = bf16[4,192,640]{2,1,0:T(8,128)(2,1)S(1)} all-to-all(bf16[4,192,640]{2,1,0:T(8,128)(2,1)S(1)} %bitcast.48), channel_id=1, replica_groups=mesh['section'=4,'seq'=8,'dp'=1] {'section'}, dimensions={0} | all-to-all | bytes 1966080 | tf_op jit(solution)/shard_map/all_to_all | solution.py:99
  237.8 0.9 reduce_sum.52
  238.7 0.0 all-gather.10.cloned.1.call-start
  238.8 24.7 %all-gather.8.cloned.1.call-done = bf16[1536,640]{1,0:T(8,128)(2,1)} async-done(((bf16[192,640]{1,0:T(8,128)(2,1)}), bf16[1536,640]{1,0:T(8,128)(2,1)}) %all-gather.8.cloned.1.call-update) | async-done | bytes 1966096 | tf_op jit(solution)/shard_map/all_gather | solution.py:102
  263.5 3.0 fusion.9
  266.5 18.9 %all_gather.17 = bf16[192,2560]{1,0:T(8,128)(2,1)S(1)} all-gather(bf16[192,640]{1,0:T(8,128)(2,1)S(1)} %copy-done.3), channel_id=1, replica_groups=mesh['section'=4,'seq'=8,'dp'=1] {'section'}, dimensions={1}, use_global_device_ids=true | all-gather | bytes 1228800 | tf_op jit(solution)/shard_map/all_gather | solution.py:101
  285.4 1.5 bitcast_convert_fusion
  286.9 11.1 %all-gather.10.cloned.1.call-done = bf16[256,2560]{0,1:T(8,128)(2,1)} async-done(((bf16[256,640]{0,1:T(8,128)(2,1)}), bf16[256,2560]{0,1:T(8,128)(2,1)}) %all-gather.10.cloned.1.call-update) | async-done | bytes 1310736 | tf_op jit(solution)/shard_map/all_gather | solution.py:107
  298.0 2.8 copy.20
  (22 shorter events, 0.1 us)
Async XLA Ops:
  7.2 256.3 %copy-start = (bf16[1,1536,256]{2,1,0:T(8,128)(2,1)S(1)}, bf16[1,1536,256]{2,1,0:T(8,128)(2,1)}, u32[]{:S(2)}) copy-start(bf16[1,1536,256]{2,1,0:T(8,128)(2,1)} %param.17) | copy-start | bytes 2359300
  7.2 6.2 %copy-start.1 = (bf16[1,192,2560]{2,1,0:T(8,128)(2,1)S(1)}, bf16[1,192,2560]{2,1,0:T(8,128)(2,1)}, u32[]{:S(2)}) copy-start(bf16[1,192,2560]{2,1,0:T(8,128)(2,1)} %param.13) | copy-start | bytes 2949124
  7.2 6.2 %copy-start.2 = (bf16[1,192,2560]{2,1,0:T(8,128)(2,1)S(1)}, bf16[1,192,2560]{2,1,0:T(8,128)(2,1)}, u32[]{:S(2)}) copy-start(bf16[1,192,2560]{2,1,0:T(8,128)(2,1)} %param.12) | copy-start | bytes 2949124
  7.2 88.1 %all-gather.6.cloned.1.call-start = ((), (), s32[]{:S(2)}) async-start(), calls=%async_computation.2 | async-start | bytes 8847360 | tf_op jit(solution)/shard_map/all_gather | solution.py:84
  11.4 2.0 copy-start.4
  13.4 1.4 copy-start.8
  14.7 197.5 %all-gather.12.cloned.1.call-start = ((), (), s32[]{:S(2)}) async-start(), calls=%async_computation.5 | async-start | bytes 11796480 | tf_op jit(solution)/shard_map/all_gather | solution.py:91
  18.0 2.5 copy-start.6
  105.1 12.4 %copy-start.7 = (f32[4]{0:T(128)S(1)}, f32[4]{0:T(128)}, u32[]{:S(2)}) copy-start(f32[4]{0:T(128)} %constant.32.clone) | copy-start | bytes 52
  113.6 98.7 %copy-start.5 = (f32[2560]{0:T(1024)S(1)}, f32[2560]{0:T(1024)}, u32[]{:S(2)}) copy-start(f32[2560]{0:T(1024)} %copy-done.4) | copy-start | bytes 30724
  113.6 47.5 %all-to-all-start = ((bf16[8,192,256]{2,1,0:T(8,128)(2,1)}), bf16[8,192,256]{2,1,0:T(8,128)(2,1)S(1)}, u32[]{:S(2)}, u32[]{:S(2)}) async-start(bf16[8,192,256]{2,1,0:T(8,128)(2,1)} %bitcast.5), calls=%async_computation | async-start | bytes 1572864 | tf_op jit(solution)/shard_map/all_to_all | solution.py:88
  117.3 146.2 %all-gather.8.cloned.1.call-start = ((), (), s32[]{:S(2)}) async-start(), calls=%async_computation.3 | async-start | bytes 2211840 | tf_op jit(solution)/shard_map/all_gather | solution.py:102
  238.7 27.8 %copy-start.3 = (bf16[192,640]{1,0:T(8,128)(2,1)S(1)}, bf16[192,640]{1,0:T(8,128)(2,1)}, u32[]{:S(2)}) copy-start(bf16[192,640]{1,0:T(8,128)(2,1)} %reduce_sum.52) | copy-start | bytes 737284
  238.7 59.3 %all-gather.10.cloned.1.call-start = ((), (), s32[]{:S(2)}) async-start(), calls=%async_computation.4 | async-start | bytes 1638400 | tf_op jit(solution)/shard_map/all_gather | solution.py:107
Sparse Core Ops, SparseCore 0:
  14.9 80.4 all-gather.5
  97.5 114.6 all-gather.11
  238.8 24.6 all-gather.7
  266.6 31.3 all-gather.9

commit v2 on v1

--- a/solution.py
+++ b/solution.py
@@ -13,6 +13,7 @@
 NEGATIVE = -1e30
 SPAN_MOST = 384
 LOG2E = 1.4426950408889634
+MESH = pl.DeviceIdType.MESH
 
 
 def attend_kernel(ids_col, ids_row, qkv, out):
@@ -62,9 +63,314 @@
     )(frame_ids[:, None], frame_ids[None, :], qkv_rows)
 
 
+def device_at(section=None, seq=None):
+    place = {}
+    if section is not None:
+        place["section"] = section
+    if seq is not None:
+        place["seq"] = seq
+    return place
+
+
+def greet(peers):
+    barrier = pltpu.get_barrier_semaphore()
+    count = 0
+    for condition, device in peers:
+        if condition is None:
+            pl.semaphore_signal(barrier, inc=1, device_id=device, device_id_type=MESH)
+            count = count + 1
+        else:
+            @pl.when(condition)
+            def _(device=device):
+                pl.semaphore_signal(barrier, inc=1, device_id=device, device_id_type=MESH)
+
+            count = count + condition.astype(jnp.int32)
+    pl.semaphore_wait(barrier, count)
+
+
+def remote(src, dst, send, recv, device):
+    return pltpu.make_async_remote_copy(
+        src_ref=src, dst_ref=dst, send_sem=send, recv_sem=recv,
+        device_id=device, device_id_type=MESH,
+    )
+
+
+def tail_kernel(
+    sections, line, finish,
+    scale, attn, w2, source, stored,
+    block_out, dmd, grad_out,
+    attn_sib, w_sib, arrived, leaving, res_out, branch, terms, parts, grads, lines, finals,
+    core_send, core_recv, sum_send, sum_recv, plane_send, plane_recv,
+    line_send, line_recv, sib_send, sib_recv,
+):
+    section = lax.axis_index("section")
+    me = lax.axis_index("seq")
+    z, core = lax.div(me, 2), lax.rem(me, 2)
+    sibling = device_at(seq=2 * z + 1 - core)
+    above = device_at(seq=jnp.minimum(me + 2, 2 * line - 1))
+    below = device_at(seq=jnp.maximum(me - 2, 0))
+    plane = [device_at(section=lax.rem(section + d, sections)) for d in range(1, sections)]
+    has_above, has_below = z < line - 1, z > 0
+    greet([(None, sibling), (has_above, above), (has_below, below)] + [(None, p) for p in plane])
+
+    rows = source.shape[0]
+    both = 2 * rows
+    half = w2.shape[2]
+    quarter = terms.shape[2]
+    tile = 256 if half % 256 == 0 else 128
+
+    w_copy = remote(w2.at[1 - core], w_sib, core_send.at[0], core_recv.at[0], sibling)
+    a_copy = remote(attn, attn_sib, core_send.at[1], core_recv.at[1], sibling)
+    w_copy.start()
+    a_copy.start()
+    w_copy.wait()
+    a_copy.wait()
+
+    def product(first, amount, column):
+        span = pl.ds(pl.multiple_of(first, rows), amount)
+        return jnp.dot(
+            attn[span, :], w2[core, :, pl.ds(column, tile)], preferred_element_type=jnp.float32
+        ) + jnp.dot(
+            attn_sib[span, :], w_sib[:, pl.ds(column, tile)], preferred_element_type=jnp.float32
+        )
+
+    def sum_copy(way, target):
+        return remote(
+            leaving.at[target], arrived.at[way, target],
+            sum_send.at[way, target], sum_recv.at[way, target],
+            above if way == 0 else below,
+        )
+
+    def push(way, target, has_before):
+        @pl.when(has_before)
+        def _():
+            sum_copy(way, target).wait_recv()
+
+        for column in range(0, half, tile):
+            value = product(target * both, both, column)
+            before = arrived[way, target, :, pl.ds(column, tile)].astype(jnp.float32)
+            value = value + jnp.where(has_before, before, 0.0)
+            leaving[target, :, pl.ds(column, tile)] = value.astype(jnp.bfloat16)
+        sum_copy(way, target).start()
+
+    def step(tau, carry):
+        @pl.when(tau >= z)
+        def _():
+            push(0, line - 1 - tau + z, has_below)
+
+        @pl.when(tau >= line - 1 - z)
+        def _():
+            push(1, tau - (line - 1 - z), has_above)
+
+        return carry
+
+    lax.fori_loop(0, line - 1, step, 0)
+
+    @pl.when(has_below)
+    def _():
+        sum_copy(0, z).wait_recv()
+
+    @pl.when(has_above)
+    def _():
+        sum_copy(1, z).wait_recv()
+
+    def own(which, store):
+        span = pl.ds(pl.multiple_of(which * rows, rows), rows)
+        for column in range(0, half, tile):
+            value = product(z * both + which * rows, rows, column)
+            up = arrived[0, z, span, pl.ds(column, tile)].astype(jnp.float32)
+            down = arrived[1, z, span, pl.ds(column, tile)].astype(jnp.float32)
+            store(column, value + jnp.where(has_below, up, 0.0) + jnp.where(has_above, down, 0.0))
+
+    def to_sibling(column, value):
+        res_out[:, pl.ds(column, tile)] = value
+
+    def to_branch(column, value):
+        branch[core, :, pl.ds(column, tile)] = value
+
+    own(1 - core, to_sibling)
+    res_copy = remote(res_out, branch.at[core], core_send.at[2], core_recv.at[2], sibling)
+    res_copy.start()
+    own(core, to_branch)
+    res_copy.wait_send()
+    remote(res_out, branch.at[1 - core], core_send.at[2], core_recv.at[2], sibling).wait_recv()
+
+    per_half = half // quarter
+    for q in range(sections):
+        low = (q % per_half) * quarter
+        terms[q] = (scale[0, 0] * branch[q // per_half, :, low:low + quarter]).astype(jnp.bfloat16)
+
+    def plane_copies(phase, src, dst):
+        return [
+            remote(src(lax.rem(section + d, sections)), dst(d),
+                   plane_send.at[phase, d - 1], plane_recv.at[phase, d - 1], plane[d - 1])
+            for d in range(1, sections)
+        ]
+
+    sends = plane_copies(0, lambda to: terms.at[to], lambda d: parts.at[d - 1])
+    for copy in sends:
+        copy.start()
+    for h in range(2):
+        columns = slice(h * half, (h + 1) * half)
+        block_out[:, columns] = (source[:, columns] + branch[h]).astype(jnp.bfloat16)
+    total = terms[section].astype(jnp.float32)
+    for d in range(1, sections):
+        sends[d - 1].wait()
+        total = total + parts[d - 1].astype(jnp.float32)
+    grad = total.astype(jnp.bfloat16)
+    lines[z, core] = grad
+    grads[section] = grad
+
+    def line_copy(way, block):
+        return remote(
+            lines.at[block, core], lines.at[block, core],
+            line_send.at[way, block], line_recv.at[way, block], above if way == 0 else below,
+        )
+
+    def sib_copy(block):
+        return remote(
+            lines.at[block, core], lines.at[block, core],
+            sib_send.at[block], sib_recv.at[block], sibling,
+        )
+
+    @pl.when(has_above)
+    def _():
+        line_copy(0, z).start()
+
+    @pl.when(has_below)
+    def _():
+        line_copy(1, z).start()
+
+    sib_copy(z).start()
+
+    def gather(phase, buffer):
+        copies = plane_copies(phase, lambda to: buffer.at[section], lambda d: buffer.at[section])
+        for copy in copies:
+            copy.start()
+        return copies
+
+    def gathered(phase, buffer, copies):
+        for d in range(1, sections):
+            copies[d - 1].wait_send()
+            slot = buffer.at[lax.rem(section + sections - d, sections)]
+            remote(slot, slot, plane_send.at[phase, d - 1], plane_recv.at[phase, d - 1],
+                   plane[d - 1]).wait_recv()
+
+    copies = gather(1, grads)
+    for k in range(1, line):
+        @pl.when(z >= k)
+        def _(k=k):
+            line_copy(0, z - k).wait_recv()
+
+            @pl.when(has_above)
+            def _():
+                line_copy(0, z - k).start()
+
+            sib_copy(z - k).start()
+
+        @pl.when(z + k < line)
+        def _(k=k):
+            line_copy(1, z + k).wait_recv()
+
+            @pl.when(has_below)
+            def _():
+                line_copy(1, z + k).start()
+
+            sib_copy(z + k).start()
+
+    def sib_wait(block, carry):
+        slot = lines.at[block, 1 - core]
+        sib_copy(block).wait_send()
+        remote(slot, slot, sib_send.at[block], sib_recv.at[block], sibling).wait_recv()
+        return carry
+
+    lax.fori_loop(0, line, sib_wait, 0)
+    everything = lines[...].reshape(line * both, quarter)
+    local = jnp.dot(stored[...], everything, preferred_element_type=jnp.float32)
+    if finish:
+        finals[section] = local.astype(jnp.bfloat16)
+        last = gather(2, finals)
+    else:
+        grad_out[...] = local
+    gathered(1, grads, copies)
+    for q in range(sections):
+        dmd[:, q * quarter:(q + 1) * quarter] = grads[q].astype(jnp.float32)
+
+    def line_drain(block, carry):
+        @pl.when(jnp.logical_and(block <= z, has_above))
+        def _():
+            line_copy(0, block).wait_send()
+
+        @pl.when(jnp.logical_and(block >= z, has_below))
+        def _():
+            line_copy(1, block).wait_send()
+
+        @pl.when(block > z)
+        def _():
+            sum_copy(0, block).wait_send()
+
+        @pl.when(block < z)
+        def _():
+            sum_copy(1, block).wait_send()
+
+        return carry
+
+    lax.fori_loop(0, line, line_drain, 0)
+    if finish:
+        gathered(2, finals, last)
+        for q in range(sections):
+            grad_out[:, q * quarter:(q + 1) * quarter] = finals[q].astype(jnp.float32)
+
+
+def tail(scale, attn, w_proj, source, stored, finish):
+    sections, seq = lax.axis_size("section"), lax.axis_size("seq")
+    line = seq // 2
+    rows, width = source.shape
+    length, inner = attn.shape
+    half, quarter = width // 2, width // sections
+    w2 = w_proj.reshape(inner, 2, half).transpose(1, 0, 2)
+    vmem = pl.BlockSpec(memory_space=pltpu.VMEM)
+    smem = pl.BlockSpec(memory_space=pltpu.SMEM)
+    bf, f32 = jnp.bfloat16, jnp.float32
+    dma = pltpu.SemaphoreType.DMA
+    return pl.pallas_call(
+        functools.partial(tail_kernel, sections, line, finish),
+        out_shape=(
+            jax.ShapeDtypeStruct((rows, width), bf),
+            jax.ShapeDtypeStruct((rows, width), f32),
+            jax.ShapeDtypeStruct((inner, width if finish else quarter), f32),
+        ),
+        in_specs=[smem] + [vmem] * 4,
+        out_specs=(vmem,) * 3,
+        scratch_shapes=[
+            pltpu.VMEM((length, inner), bf),
+            pltpu.VMEM((inner, half), bf),
+            pltpu.VMEM((2, line, 2 * rows, half), bf),
+            pltpu.VMEM((line, 2 * rows, half), bf),
+            pltpu.VMEM((rows, half), f32),
+            pltpu.VMEM((2, rows, half), f32),
+            pltpu.VMEM((sections, rows, quarter), bf),
+            pltpu.VMEM((sections - 1, rows, quarter), bf),
+            pltpu.VMEM((sections, rows, quarter), bf),
+            pltpu.VMEM((line, 2, rows, quarter), bf),
+            pltpu.VMEM((sections, inner, quarter), bf),
+            dma((3,)), dma((3,)),
+            dma((2, line)), dma((2, line)),
+            dma((3, sections - 1)), dma((3, sections - 1)),
+            dma((2, line)), dma((2, line)),
+            dma((line,)), dma((line,)),
+        ],
+        compiler_params=pltpu.CompilerParams(
+            collective_id=1, has_side_effects=True, vmem_limit_bytes=56 << 20
+        ),
+        cost_estimate=pl.CostEstimate(
+            flops=2 * length * inner * width, bytes_accessed=8 << 20, transcendentals=0
+        ),
+    )(scale, attn, w2, source, stored)
+
+
 def per_device(roles, block_ids, latent, pending, context, w_qkv, w_out, stored_attn):
     section = lax.axis_index("section")
-    sections = lax.axis_size("section")
     places = jnp.arange(4, dtype=jnp.int32)
     weight_table = jnp.array([0.0, -GUIDE, GUIDE - 1.0, 1.0], jnp.float32)
     section_role = jnp.sum(jnp.where(places == section, roles, 0))
@@ -74,7 +380,6 @@
     w_proj = lax.dynamic_index_in_dim(w_out, model_index, 0, keepdims=False)
     is_generator = section_role == 0
     with_context = jnp.logical_or(section_role == 1, section_role == 3).astype(jnp.float32)
-    width = latent.shape[2]
     scored = pending[0].astype(jnp.float32) + with_context * context[0][None, :]
     source = jnp.where(is_generator, latent[0].astype(jnp.float32), scored)
     normed = (
@@ -85,27 +390,14 @@
     ).astype(jnp.bfloat16)
     frame_ids = jnp.where(is_generator, block_ids[0, 0], block_ids[1, 0])
     attn = attend(qkv_rows, frame_ids)
-    local_attn = lax.all_to_all(attn, "seq", split_axis=0, concat_axis=1, tiled=True)
-    branch = jnp.dot(
-        local_attn,
-        lax.all_gather(w_proj, "seq", axis=0, tiled=True),
-        preferred_element_type=jnp.float32,
+    finish = lax.axis_size("dp") == 1
+    block_out, gradient, grad_out = tail(
+        score_weight.reshape(1, 1), attn, w_proj, source, stored_attn[0].T, finish
     )
-    block_out = (source + branch).astype(jnp.bfloat16)[None, None]
-    rows = branch.shape[0]
-    quarter = width // sections
-    terms = (score_weight * branch).astype(jnp.bfloat16)
-    terms = terms.reshape(rows, sections, quarter).transpose(1, 0, 2)
-    terms = lax.all_to_all(terms, "section", split_axis=0, concat_axis=0, tiled=True)
-    grad_bf = jnp.sum(terms.astype(jnp.float32), axis=0).astype(jnp.bfloat16)
-    gradient = lax.all_gather(grad_bf, "section", axis=1, tiled=True).astype(jnp.float32)
-    grad_rows = lax.all_gather(grad_bf, "seq", axis=0, tiled=True)
-    local_grad = lax.dot_general(
-        stored_attn[0], grad_rows, (((0,), (0,)), ((), ())), preferred_element_type=jnp.float32
-    )
-    local_grad = lax.psum(local_grad, "dp").astype(jnp.bfloat16)
-    grad_out = lax.all_gather(local_grad, "section", axis=1, tiled=True).astype(jnp.float32)
-    return (block_out, gradient[None], grad_out)
+    if not finish:
+        grad_out = lax.psum(grad_out, "dp").astype(jnp.bfloat16)
+        grad_out = lax.all_gather(grad_out, "section", axis=1, tiled=True).astype(jnp.float32)
+    return (block_out[None, None], gradient[None], grad_out)
 
 
 def solution(mesh):

time: 308 us -> 262 us (0.85)
  Pallas kernels: 8.5 us -> 143 us
  waiting for transfers between devices: 202 us -> 71.2 us
  blocking collectives: 36.3 us -> 0 us
  matrix products: 20.7 us -> 9.75 us
  local copies, waits for them, and re-layouts: 6.69 us -> 12.2 us
  starting transfers between devices: 4.02 us -> 0.04 us
  other arithmetic: 11.1 us -> 7.64 us
    pallas_call x0 -> x1, Pallas kernels: none -> 135 us  [tail(): pl.pallas_call(functools.partial(tail_kernel, sections, line, finish), ou...]
    all_gather x3 -> x0, waiting for transfers between devices: 86.1 us -> none  [the longest x1 50.2 us: per_device(): lax.all_gather(w_proj, 'seq', axis=0, tiled=True)]
    all_to_all x1 -> x0, waiting for transfers between devices: 42.4 us -> none  [per_device(): lax.all_to_all(attn, 'seq', split_axis=0, concat_axis=1, tiled=True)]
    all_gather x1 -> x0, blocking collectives: 18.9 us -> none  [per_device(): lax.all_gather(grad_bf, 'section', axis=1, tiled=True).astype(jnp.float32)]
    all_to_all x1 -> x0, blocking collectives: 17.5 us -> none  [per_device(): lax.all_to_all(terms, 'section', split_axis=0, concat_axis=0, tiled=True)]
    dot_general x2 -> x0, matrix products: 11 us -> none  [the longest x1 7.97 us: per_device(): jnp.dot(local_attn, lax.all_gather(w_proj, 'seq', axis=0, tiled=True), pr...]
    unnamed x19 -> x21, local copies, waits for them, and re-layouts: 2.87 us -> 9.02 us
    all_to_all x1 -> x0, starting transfers between devices: 3.68 us -> none  [per_device(): lax.all_to_all(attn, 'seq', split_axis=0, concat_axis=1, tiled=True)]
  transfers between devices with their start and end apart: 5 -> 1, of which waited for: 5 -> 1; matrix products, arithmetic and copies ran while one was open for 6% -> 3% of each run, Pallas kernels for 3% -> 0%
where the time goes in v2:
time: 262 us; the launch traced here: 261 us
  Pallas kernels  143 us (55%)
  waiting for transfers between devices  71.2 us (27%)
  between operations  17.8 us (7%)
  local copies, waits for them, and re-layouts  12.2 us (5%)
  matrix products  9.75 us (4%)
  other arithmetic  7.64 us (3%)
    pallas_call x1, Pallas kernels, tail(): pl.pallas_call(functools.partial(tail_kernel, sections, line, finish), ou...  135 us
    all_gather x1, waiting for transfers between devices, per_device(): lax.all_gather(normed, 'seq', axis=0, tiled=True)  71.2 us
    dot_general x1, matrix products, per_device(): jnp.dot(lax.all_gather(normed, 'seq', axis=0, tiled=True), w_in, preferre...  9.75 us
    unnamed x21, local copies, waits for them, and re-layouts  9.02 us
    pallas_call x1, Pallas kernels, attend(): pl.pallas_call(attend_kernel, out_shape=jax.ShapeDtypeStruct((length, hea...  7.61 us
  transfers between devices with their start and end apart: 1, of which 1 were waited for; matrix products, arithmetic and copies ran while one was open for 3% of the time, Pallas kernels for 0%

profile of v2, /device:TPU:0, one launch (start us, length us, event | category | flops | bytes accessed | tf_op | source)
XLA Modules:
  0.0 261.4 jit_solution(10390619601442493555)
XLA Ops:
  7.2 0.0 all-gather.2.cloned.1.call-start
  7.2 1.3 fusion.9
  10.2 0.7 multiply_reduce_fusion.1
  10.9 2.0 multiply_reduce_fusion
  12.9 0.0 copy-start.7
  12.9 0.0 copy-start.5
  13.0 1.3 multiply_convert_fusion
  14.2 0.0 all-gather.2.cloned.1.call-update
  14.2 0.0 copy-done.7
  14.2 1.2 fusion.8
  16.7 0.0 copy-done.5
  16.8 0.3 copy.14.ids_col
  17.1 0.0 copy-done.1
  17.7 1.4 constant_dynamic-slice_fusion
  19.1 0.6 copy.18
  19.8 0.0 copy-start.4
  19.8 0.0 copy-start.6
  19.8 1.4 copy.16
  21.2 0.0 copy-done.4
  21.2 1.2 copy.17
  22.4 1.2 fusion.7
  23.6 71.2 %all-gather.2.cloned.1.call-done = bf16[1536,2560]{1,0:T(8,128)(2,1)} async-done(((bf16[192,2560]{1,0:T(8,128)(2,1)}), bf16[1536,2560]{1,0:T(8,128)(2,1)}) %all-gather.2.cloned.1.call-update) | async-done | bytes 7864336 | tf_op jit(solution)/shard_map/all_gather | solution.py:389
  94.8 9.7 %fusion.3.qkv = bf16[1536,768]{1,0:T(8,128)(2,1)S(1)} fusion(bf16[1536,2560]{1,0:T(8,128)(2,1)} %all-gather.2.cloned.1.call-done, bf16[3,2560,768]{2,1,0:T(8,128)(2,1)} %param.15, s32[]{:T(128)S(6)} %select_n.63), kind=kOutput, calls=%fused_computation.3 | convolution fusion | flops 6040977408 | bytes 14155780 | tf_op jit(solution)/shard_map/dot_general | solution.py:388
  104.6 7.6 %shard_map.121.attn = bf16[1536,256]{1,0:T(8,128)(2,1)S(1)} custom-call(s32[1536,1]{1,0:T(8,128)S(1)} %copy.14.ids_col, s32[1,1536]{1,0:T(1,128)S(1)} %fusion.13.ids_row, bf16[1536,768]{1,0:T(8,128)(2,1)S(1)} %fusion.3.qkv), custom_call_target="tpu_custom_call" | custom-call | flops 2415919104 | bytes 3538944 | tf_op jit(solution)/shard_map/pallas_call | solution.py:52
  112.2 0.0 copy-start
  112.2 0.9 copy-done
  113.1 135.2 %shard_map.122 = (bf16[192,2560]{1,0:T(8,128)(2,1)}, f32[192,2560]{1,0:T(8,128)}, f32[256,2560]{1,0:T(8,128)}) custom-call(f32[1,1]{1,0:T(1,128)} %bitcast.scale, bf16[1536,256]{1,0:T(8,128)(2,1)} %copy-done, bf16[2,256,1280]{2,1,0:T(8,128)(2,1)} %bitcast.28, f32[192,2560]{1,0:T(8,128)} %copy-done.1, bf16[256,1536]{1,0:T(8,128)(2,1)} %bitcast.30), custom_call_target="tpu_custom_call" | custom-call | flops 2013265920 | bytes 8388608 | tf_op jit(solution)/shard_map/pallas_call | solution.py:336
  248.3 0.0 copy-start.3
  248.3 2.4 copy.22
  250.6 1.3 copy.23
  251.9 1.2 copy-done.2
  253.1 1.5 copy.24
  (7 shorter events, 0.0 us)
Async XLA Ops:
  7.2 87.7 %all-gather.2.cloned.1.call-start = ((), (), s32[]{:S(2)}) async-start(), calls=%async_computation | async-start | bytes 8847360 | tf_op jit(solution)/shard_map/all_gather | solution.py:389
  12.9 4.2 %copy-start.1 = (f32[192,2560]{1,0:T(8,128)}, f32[192,2560]{1,0:T(8,128)S(1)}, u32[]{:S(2)}) copy-start(f32[192,2560]{1,0:T(8,128)S(1)} %get-tuple-element.10.source) | copy-start | bytes 5898244
  12.9 1.3 copy-start.7
  12.9 3.8 %copy-start.5 = (s32[2,1,1536]{2,1,0:T(1,128)S(1)}, s32[2,1,1536]{2,1,0:T(1,128)}, u32[]{:S(2)}) copy-start(s32[2,1,1536]{2,1,0:T(1,128)} %param.11) | copy-start | bytes 36868
  19.8 1.5 copy-start.4
  19.8 2.7 %copy-start.6 = (f32[4]{0:T(128)S(1)}, f32[4]{0:T(128)}, u32[]{:S(2)}) copy-start(f32[4]{0:T(128)} %constant.30.clone) | copy-start | bytes 52
  112.2 0.9 copy-start
  248.3 2.4 copy-start.3
  250.6 2.5 copy-start.2
Sparse Core Ops, SparseCore 0:
  14.4 80.4 all-gather.1

commit v3 on v2

--- a/solution.py
+++ b/solution.py
@@ -95,9 +95,217 @@
     )
 
 
+def head_kernel(
+    sections, line,
+    flags, latent, pending, context, w_in, qkv,
+    inbox, full, outbox,
+    z_send, z_recv, plane_send, plane_recv, sib_send, sib_recv, slab_send, slab_recv,
+):
+    section = lax.axis_index("section")
+    me = lax.axis_index("seq")
+    z, core = lax.div(me, 2), lax.rem(me, 2)
+    sibling = device_at(seq=2 * z + 1 - core)
+    above = device_at(seq=jnp.minimum(me + 2, 2 * line - 1))
+    below = device_at(seq=jnp.maximum(me - 2, 0))
+    plane = [device_at(section=lax.rem(section + d, sections)) for d in range(1, sections)]
+    has_above, has_below = z < line - 1, z > 0
+    greet([(None, sibling), (has_above, above), (has_below, below)] + [(None, p) for p in plane])
+
+    pieces, chunk = inbox.shape[1], inbox.shape[3]
+
+    def z_copy(way, block, h):
+        return remote(
+            inbox.at[block, h], inbox.at[block, h], z_send.at[way, block, h],
+            z_recv.at[block, h], above if way == 0 else below,
+        )
+
+    for h in range(pieces):
+        rows = pl.ds(pl.multiple_of((section * pieces + h) * chunk, chunk), chunk)
+        inbox[z, h, 0] = latent[rows, :]
+        inbox[z, h, 1] = pending[rows, :]
+
+        @pl.when(has_above)
+        def _(h=h):
+            z_copy(0, z, h).start()
+
+        @pl.when(has_below)
+        def _(h=h):
+            z_copy(1, z, h).start()
+
+    def normed(latent_rows, pending_rows, to):
+        source = source_of(flags, context, latent_rows, pending_rows, to)
+        mean = jnp.mean(source * source, axis=1, keepdims=True)
+        return (source * lax.rsqrt(mean + EPSILON)).astype(jnp.bfloat16)
+
+    def own(index, carry):
+        q, h = lax.div(index, pieces), lax.rem(index, pieces)
+        rows = pl.ds(pl.multiple_of(index * chunk, chunk), chunk)
+        full[z, core, q, h] = normed(latent[rows, :], pending[rows, :], section)
+        return carry
+
+    lax.fori_loop(0, sections * pieces, own, 0)
+
+    def slab_copy(owner):
+        return remote(full.at[z, owner], full.at[z, owner], slab_send, slab_recv, sibling)
+
+    slab_copy(core).start()
+
+    def plane_copy(d, block, h, owner):
+        return remote(
+            outbox.at[d - 1, block, h], full.at[block, core, owner, h],
+            plane_send.at[d - 1, block, h], plane_recv.at[d - 1, block, h], plane[d - 1],
+        )
+
+    def sib_copy(block, q, h, owner):
+        slot = full.at[block, owner, q, h]
+        return remote(slot, slot, sib_send.at[block, q, h], sib_recv.at[block, q, h], sibling)
+
+    def multiply(block):
+        rows = full[block].reshape(2 * sections * pieces * chunk, full.shape[-1])
+        place = pl.ds(pl.multiple_of(block * rows.shape[0], rows.shape[0]), rows.shape[0])
+        for column in range(0, qkv.shape[1], 128):
+            qkv[place, column:column + 128] = jnp.dot(
+                rows, w_in[:, column:column + 128], preferred_element_type=jnp.float32
+            ).astype(jnp.bfloat16)
+
+    def take(block, h, way, onward):
+        z_copy(way, block, h).wait_recv()
+
+        @pl.when(onward)
+        def _():
+            z_copy(way, block, h).start()
+
+        latent_rows, pending_rows = inbox[block, h, 0], inbox[block, h, 1]
+        for d in range(1, sections):
+            outbox[d - 1, block, h] = normed(
+                latent_rows, pending_rows, lax.rem(section + d, sections)
+            )
+            plane_copy(d, block, h, section).start()
+        full[block, core, section, h] = normed(latent_rows, pending_rows, section)
+        sib_copy(block, section, h, core).start()
+
+    def pass_on(block, h):
+        for d in range(1, sections):
+            sender = lax.rem(section + sections - d, sections)
+            plane_copy(d, block, h, sender).wait_recv()
+            sib_copy(block, sender, h, core).start()
+
+    def finish(block):
+        for h in range(pieces):
+            for q in range(sections):
+                sib_copy(block, q, h, 1 - core).wait_recv()
+        multiply(block)
+
+    def step(index, carry):
+        k, h = lax.div(index, pieces), lax.rem(index, pieces)
+
+        @pl.when(jnp.logical_and(k < line, z >= k))
+        def _():
+            take(z - k, h, 0, has_above)
+
+        @pl.when(z + k < line)
+        def _():
+            take(z + k, h, 1, has_below)
+
+        late = index - 2
+        k2, h2 = lax.div(late, pieces), lax.rem(late, pieces)
+
+        @pl.when(jnp.logical_and(k2 >= 1, z >= k2))
+        def _():
+            pass_on(z - k2, h2)
+
+        @pl.when(jnp.logical_and(k2 >= 1, z + k2 < line))
+        def _():
+            pass_on(z + k2, h2)
+
+        done = k - 1
+
+        @pl.when(h == 1)
+        def _():
+            @pl.when(done == 0)
+            def _():
+                slab_copy(1 - core).wait_recv()
+                multiply(z)
+
+            @pl.when(jnp.logical_and(done >= 1, z >= done))
+            def _():
+                finish(z - done)
+
+            @pl.when(jnp.logical_and(done >= 1, z + done < line))
+            def _():
+                finish(z + done)
+
+        return carry
+
+    lax.fori_loop(pieces, line * pieces + 2, step, 0)
+
+    slab_copy(core).wait_send()
+
+    def drain(index, carry):
+        block, h = lax.div(index, pieces), lax.rem(index, pieces)
+
+        @pl.when(jnp.logical_and(block <= z, has_above))
+        def _():
+            z_copy(0, block, h).wait_send()
+
+        @pl.when(jnp.logical_and(block >= z, has_below))
+        def _():
+            z_copy(1, block, h).wait_send()
+
+        @pl.when(block != z)
+        def _():
+            for d in range(1, sections):
+                plane_copy(d, block, h, section).wait_send()
+            for q in range(sections):
+                sib_copy(block, q, h, core).wait_send()
+
+        return carry
+
+    lax.fori_loop(0, line * pieces, drain, 0)
+
+
+def head(flags, latent, pending, context, w_in):
+    sections, seq = lax.axis_size("section"), lax.axis_size("seq")
+    line = seq // 2
+    rows, width = latent.shape
+    chunk = 16
+    pieces = rows // (sections * chunk)
+    vmem = pl.BlockSpec(memory_space=pltpu.VMEM)
+    smem = pl.BlockSpec(memory_space=pltpu.SMEM)
+    dma = pltpu.SemaphoreType.DMA
+    bf = jnp.bfloat16
+    return pl.pallas_call(
+        functools.partial(head_kernel, sections, line),
+        out_shape=jax.ShapeDtypeStruct((seq * rows, w_in.shape[1]), bf),
+        in_specs=[smem] + [vmem] * 4,
+        out_specs=vmem,
+        scratch_shapes=[
+            pltpu.VMEM((line, pieces, 2, chunk, width), bf),
+            pltpu.VMEM((line, 2, sections, pieces, chunk, width), bf),
+            pltpu.VMEM((sections - 1, line, pieces, chunk, width), bf),
+            dma((2, line, pieces)), dma((line, pieces)),
+            dma((sections - 1, line, pieces)), dma((sections - 1, line, pieces)),
+            dma((line, sections, pieces)), dma((line, sections, pieces)),
+            dma(()), dma(()),
+        ],
+        compiler_params=pltpu.CompilerParams(
+            collective_id=2, has_side_effects=True, vmem_limit_bytes=56 << 20
+        ),
+        cost_estimate=pl.CostEstimate(
+            flops=2 * seq * rows * w_in.size, bytes_accessed=16 << 20, transcendentals=0
+        ),
+    )(flags, latent, pending, context, w_in)
+
+
+def source_of(flags, context, latent_rows, pending_rows, to):
+    scored = pending_rows.astype(jnp.float32) + flags[1, to] * context[...]
+    generator = flags[0, to]
+    return generator * latent_rows.astype(jnp.float32) + (1.0 - generator) * scored
+
+
 def tail_kernel(
     sections, line, finish,
-    scale, attn, w2, source, stored,
+    scale, flags, attn, w2, latent, pending, context, stored,
     block_out, dmd, grad_out,
     attn_sib, w_sib, arrived, leaving, res_out, branch, terms, parts, grads, lines, finals,
     core_send, core_recv, sum_send, sum_recv, plane_send, plane_recv,
@@ -113,7 +321,7 @@
     has_above, has_below = z < line - 1, z > 0
     greet([(None, sibling), (has_above, above), (has_below, below)] + [(None, p) for p in plane])
 
-    rows = source.shape[0]
+    rows = latent.shape[0]
     both = 2 * rows
     half = w2.shape[2]
     quarter = terms.shape[2]
@@ -210,6 +418,7 @@
     sends = plane_copies(0, lambda to: terms.at[to], lambda d: parts.at[d - 1])
     for copy in sends:
         copy.start()
+    source = source_of(flags, context, latent[...], pending[...], section)
     for h in range(2):
         columns = slice(h * half, (h + 1) * half)
         block_out[:, columns] = (source[:, columns] + branch[h]).astype(jnp.bfloat16)
@@ -322,10 +531,10 @@
             grad_out[:, q * quarter:(q + 1) * quarter] = finals[q].astype(jnp.float32)
 
 
-def tail(scale, attn, w_proj, source, stored, finish):
+def tail(scale, flags, attn, w_proj, latent, pending, context, stored, finish):
     sections, seq = lax.axis_size("section"), lax.axis_size("seq")
     line = seq // 2
-    rows, width = source.shape
+    rows, width = latent.shape
     length, inner = attn.shape
     half, quarter = width // 2, width // sections
     w2 = w_proj.reshape(inner, 2, half).transpose(1, 0, 2)
@@ -340,7 +549,7 @@
             jax.ShapeDtypeStruct((rows, width), f32),
             jax.ShapeDtypeStruct((inner, width if finish else quarter), f32),
         ),
-        in_specs=[smem] + [vmem] * 4,
+        in_specs=[smem] * 2 + [vmem] * 6,
         out_specs=(vmem,) * 3,
         scratch_shapes=[
             pltpu.VMEM((length, inner), bf),
@@ -366,7 +575,7 @@
         cost_estimate=pl.CostEstimate(
             flops=2 * length * inner * width, bytes_accessed=8 << 20, transcendentals=0
         ),
-    )(scale, attn, w2, source, stored)
+    )(scale, flags, attn, w2, latent, pending, context, stored)
 
 
 def per_device(roles, block_ids, latent, pending, context, w_qkv, w_out, stored_attn):
@@ -379,20 +588,16 @@
     w_in = lax.dynamic_index_in_dim(w_qkv, model_index, 0, keepdims=False)
     w_proj = lax.dynamic_index_in_dim(w_out, model_index, 0, keepdims=False)
     is_generator = section_role == 0
-    with_context = jnp.logical_or(section_role == 1, section_role == 3).astype(jnp.float32)
-    scored = pending[0].astype(jnp.float32) + with_context * context[0][None, :]
-    source = jnp.where(is_generator, latent[0].astype(jnp.float32), scored)
-    normed = (
-        source * lax.rsqrt(jnp.mean(source * source, axis=1, keepdims=True) + EPSILON)
-    ).astype(jnp.bfloat16)
-    qkv_rows = jnp.dot(
-        lax.all_gather(normed, "seq", axis=0, tiled=True), w_in, preferred_element_type=jnp.float32
-    ).astype(jnp.bfloat16)
+    flags = jnp.stack(
+        [roles == 0, jnp.logical_or(roles == 1, roles == 3)]
+    ).astype(jnp.float32)
+    qkv_rows = head(flags, latent[0], pending[0], context, w_in)
     frame_ids = jnp.where(is_generator, block_ids[0, 0], block_ids[1, 0])
     attn = attend(qkv_rows, frame_ids)
     finish = lax.axis_size("dp") == 1
     block_out, gradient, grad_out = tail(
-        score_weight.reshape(1, 1), attn, w_proj, source, stored_attn[0].T, finish
+        score_weight.reshape(1, 1), flags, attn, w_proj, latent[0], pending[0], context,
+        stored_attn[0].T, finish,
     )
     if not finish:
         grad_out = lax.psum(grad_out, "dp").astype(jnp.bfloat16)

time: 262 us -> 227 us (0.87)
  waiting for transfers between devices: 71.2 us -> 0 us
  Pallas kernels: 143 us -> 202 us
  between operations: 17.8 us -> 3.36 us
  matrix products: 9.75 us -> 0 us
  local copies, waits for them, and re-layouts: 12.2 us -> 16.8 us
    all_gather x1 -> x0, waiting for transfers between devices: 71.2 us -> none  [per_device(): lax.all_gather(normed, 'seq', axis=0, tiled=True)]
    pallas_call x0 -> x1, Pallas kernels: none -> 59.1 us  [head(): pl.pallas_call(functools.partial(head_kernel, sections, line), out_shape=...]
    dot_general x1 -> x0, matrix products: 9.75 us -> none  [per_device(): jnp.dot(lax.all_gather(normed, 'seq', axis=0, tiled=True), w_in, preferre...]
    squeeze x0 -> x1, local copies, waits for them, and re-layouts: none -> 4.24 us  [per_device(): w_in = lax.dynamic_index_in_dim(w_qkv, model_index, 0, keepdims=False)]
  transfers between devices with their start and end apart: 1 -> 0, of which waited for: 1 -> 0; matrix products, arithmetic and copies ran while one was open for 3% -> 0% of each run, Pallas kernels for 0% -> 0%
where the time goes in v3:
time: 227 us
  Pallas kernels  202 us (89%)
  local copies, waits for them, and re-layouts  16.8 us (7%)
  other arithmetic  5.14 us (2%)
  between operations  3.36 us (1%)
    pallas_call x1, Pallas kernels, tail(): pl.pallas_call(functools.partial(tail_kernel, sections, line, finish), ou...  135 us
    pallas_call x1, Pallas kernels, head(): pl.pallas_call(functools.partial(head_kernel, sections, line), out_shape=...  59.1 us
    unnamed x21, local copies, waits for them, and re-layouts  9.45 us
    pallas_call x1, Pallas kernels, attend(): pl.pallas_call(attend_kernel, out_shape=jax.ShapeDtypeStruct((length, hea...  7.94 us

profile of v3, /device:TPU:0, one launch (start us, length us, event | category | flops | bytes accessed | tf_op | source)
XLA Modules:
  0.0 226.9 jit_solution(11318222170525397653)
XLA Ops:
  0.6 1.3 fusion.2
  1.9 1.9 fusion.1
  5.8 0.0 copy-start.6
  5.8 4.2 %dynamic-slice_bitcast_fusion.w_in = bf16[2560,768]{1,0:T(8,128)(2,1)} fusion(bf16[3,2560,768]{2,1,0:T(8,128)(2,1)} %param.15, s32[]{:T(128)S(6)} %select_n.53), kind=kLoop, calls=%fused_computation | loop fusion | bytes 7864324 | tf_op jit(solution)/shard_map/jit(dynamic_index_in_dim)/squeeze | solution.py:588
  10.1 0.0 copy-done.6
  10.1 0.6 add_convert_fusion.flags
  10.7 0.0 copy-start.5
  10.7 59.1 %shard_map.121.qkv = bf16[1536,768]{1,0:T(8,128)(2,1)} custom-call(f32[2,4]{1,0:T(2,128)} %add_convert_fusion.flags, bf16[192,2560]{1,0:T(8,128)(2,1)} %bitcast.25, bf16[192,2560]{1,0:T(8,128)(2,1)} %bitcast.27, f32[1,2560]{1,0:T(1,128)} %context.3, bf16[2560,768]{1,0:T(8,128)(2,1)} %dynamic-slice_bitcast_fusion.w_in), custom_call_target="tpu_custom_call" | custom-call | flops 6039797760 | bytes 16777216 | tf_op jit(solution)/shard_map/pallas_call | solution.py:277
  70.4 0.0 copy-done.5
  70.5 0.3 copy.14.ids_col
  70.8 0.0 copy-start.1
  70.8 1.7 copy-done.1
  72.4 7.9 %shard_map.122.attn = bf16[1536,256]{1,0:T(8,128)(2,1)S(1)} custom-call(s32[1536,1]{1,0:T(8,128)S(1)} %copy.14.ids_col, s32[1,1536]{1,0:T(1,128)S(1)} %fusion.3.ids_row, bf16[1536,768]{1,0:T(8,128)(2,1)S(1)} %copy-done.1), custom_call_target="tpu_custom_call" | custom-call | flops 2415919104 | bytes 3538944 | tf_op jit(solution)/shard_map/pallas_call | solution.py:52
  80.4 0.0 copy-start
  80.4 0.9 copy-done
  81.3 1.4 constant_dynamic-slice_fusion
  82.7 0.0 copy-start.7
  82.7 0.0 copy-start.4
  82.7 0.6 copy.18
  83.3 1.4 copy.16
  84.8 0.0 copy-done.7
  84.8 1.3 fusion
  86.1 0.0 copy-done.4
  86.1 1.2 copy.17
  87.2 134.6 %shard_map.123 = (bf16[192,2560]{1,0:T(8,128)(2,1)}, f32[192,2560]{1,0:T(8,128)}, f32[256,2560]{1,0:T(8,128)}) custom-call(f32[1,1]{1,0:T(1,128)} %bitcast.scale, f32[2,4]{1,0:T(2,128)} %add_convert_fusion.flags, bf16[1536,256]{1,0:T(8,128)(2,1)} %copy-done, bf16[2,256,1280]{2,1,0:T(8,128)(2,1)} %bitcast.22, bf16[192,2560]{1,0:T(8,128)(2,1)} %bitcast.26, ...), custom_call_target="tpu_custom_call" | custom-call | flops 2013265920 | bytes 8388608 | tf_op jit(solution)/shard_map/pallas_call | solution.py:545
  221.8 0.0 copy-start.3
  221.8 0.0 copy-start.2
  221.8 2.4 %copy.22 = bf16[1,1,192,2560]{3,2,1,0:T(8,128)(2,1)} copy(bf16[1,1,192,2560]{3,2,1,0:T(8,128)(2,1)} %bitcast.23) | data formatting | bytes 1966080
  224.2 0.0 copy-done.3
  224.2 1.3 copy.23
  225.4 0.0 copy-done.2
  225.4 1.5 copy.24
  (3 shorter events, 0.0 us)
Async XLA Ops:
  5.8 4.3 %copy-start.6 = (s32[4]{0:T(128)S(1)}, s32[4]{0:T(128)}, u32[]{:S(2)}) copy-start(s32[4]{0:T(128)} %param.10) | copy-start | bytes 52
  10.7 59.8 %copy-start.5 = (s32[2,1,1536]{2,1,0:T(1,128)S(1)}, s32[2,1,1536]{2,1,0:T(1,128)}, u32[]{:S(2)}) copy-start(s32[2,1,1536]{2,1,0:T(1,128)} %param.11) | copy-start | bytes 36868
  70.8 1.7 copy-start.1
  80.4 0.9 copy-start
  82.7 2.1 copy-start.7
  82.7 3.4 %copy-start.4 = (bf16[1,1536,256]{2,1,0:T(8,128)(2,1)S(1)}, bf16[1,1536,256]{2,1,0:T(8,128)(2,1)}, u32[]{:S(2)}) copy-start(bf16[1,1536,256]{2,1,0:T(8,128)(2,1)} %param.17) | copy-start | bytes 2359300
  221.8 2.4 %copy-start.3 = (f32[192,2560]{1,0:T(8,128)S(1)}, f32[192,2560]{1,0:T(8,128)}, u32[]{:S(2)}) copy-start(f32[192,2560]{1,0:T(8,128)} %get-tuple-element.7) | copy-start | bytes 5898244
  221.8 3.6 %copy-start.2 = (f32[256,2560]{1,0:T(8,128)S(1)}, f32[256,2560]{1,0:T(8,128)}, u32[]{:S(2)}) copy-start(f32[256,2560]{1,0:T(8,128)} %get-tuple-element.16) | copy-start | bytes 7864324

commit v4 on v3

--- a/solution.py
+++ b/solution.py
@@ -325,7 +325,20 @@
     both = 2 * rows
     half = w2.shape[2]
     quarter = terms.shape[2]
-    tile = 256 if half % 256 == 0 else 128
+    per_half = half // quarter
+    tiles = quarter // 128
+    chunks = min(3, tiles)
+    edges = [128 * -(-tiles * j // chunks) for j in range(chunks + 1)]
+    widths = [edges[j + 1] - edges[j] for j in range(chunks)]
+
+    def lanes(j):
+        return slice(edges[j], edges[j + 1])
+
+    def packed(j, part=None):
+        if part is None:
+            return slice(per_half * edges[j], per_half * edges[j + 1])
+        first = per_half * edges[j] + part * widths[j]
+        return slice(first, first + widths[j])
 
     w_copy = remote(w2.at[1 - core], w_sib, core_send.at[0], core_recv.at[0], sibling)
     a_copy = remote(attn, attn_sib, core_send.at[1], core_recv.at[1], sibling)
@@ -334,201 +347,240 @@
     w_copy.wait()
     a_copy.wait()
 
-    def product(first, amount, column):
+    def product(first, amount, j, part):
         span = pl.ds(pl.multiple_of(first, rows), amount)
+        columns = slice(part * quarter + edges[j], part * quarter + edges[j + 1])
         return jnp.dot(
-            attn[span, :], w2[core, :, pl.ds(column, tile)], preferred_element_type=jnp.float32
+            attn[span, :], w2[core, :, columns], preferred_element_type=jnp.float32
         ) + jnp.dot(
-            attn_sib[span, :], w_sib[:, pl.ds(column, tile)], preferred_element_type=jnp.float32
+            attn_sib[span, :], w_sib[:, columns], preferred_element_type=jnp.float32
         )
 
-    def sum_copy(way, target):
+    def sum_copy(j, way, target):
         return remote(
-            leaving.at[target], arrived.at[way, target],
-            sum_send.at[way, target], sum_recv.at[way, target],
+            leaving.at[target, :, packed(j)], arrived.at[way, target, :, packed(j)],
+            sum_send.at[j, way, target], sum_recv.at[j, way, target],
             above if way == 0 else below,
         )
 
-    def push(way, target, has_before):
+    def push(j, way, target, has_before):
         @pl.when(has_before)
         def _():
-            sum_copy(way, target).wait_recv()
-
-        for column in range(0, half, tile):
-            value = product(target * both, both, column)
-            before = arrived[way, target, :, pl.ds(column, tile)].astype(jnp.float32)
+            sum_copy(j, way, target).wait_recv()
+
+        for part in range(per_half):
+            value = product(target * both, both, j, part)
+            before = arrived[way, target, :, packed(j, part)].astype(jnp.float32)
             value = value + jnp.where(has_before, before, 0.0)
-            leaving[target, :, pl.ds(column, tile)] = value.astype(jnp.bfloat16)
-        sum_copy(way, target).start()
-
-    def step(tau, carry):
-        @pl.when(tau >= z)
-        def _():
-            push(0, line - 1 - tau + z, has_below)
-
-        @pl.when(tau >= line - 1 - z)
-        def _():
-            push(1, tau - (line - 1 - z), has_above)
-
-        return carry
-
-    lax.fori_loop(0, line - 1, step, 0)
-
-    @pl.when(has_below)
-    def _():
-        sum_copy(0, z).wait_recv()
-
-    @pl.when(has_above)
-    def _():
-        sum_copy(1, z).wait_recv()
-
-    def own(which, store):
-        span = pl.ds(pl.multiple_of(which * rows, rows), rows)
-        for column in range(0, half, tile):
-            value = product(z * both + which * rows, rows, column)
-            up = arrived[0, z, span, pl.ds(column, tile)].astype(jnp.float32)
-            down = arrived[1, z, span, pl.ds(column, tile)].astype(jnp.float32)
-            store(column, value + jnp.where(has_below, up, 0.0) + jnp.where(has_above, down, 0.0))
-
-    def to_sibling(column, value):
-        res_out[:, pl.ds(column, tile)] = value
-
-    def to_branch(column, value):
-        branch[core, :, pl.ds(column, tile)] = value
-
-    own(1 - core, to_sibling)
-    res_copy = remote(res_out, branch.at[core], core_send.at[2], core_recv.at[2], sibling)
-    res_copy.start()
-    own(core, to_branch)
-    res_copy.wait_send()
-    remote(res_out, branch.at[1 - core], core_send.at[2], core_recv.at[2], sibling).wait_recv()
-
-    per_half = half // quarter
-    for q in range(sections):
-        low = (q % per_half) * quarter
-        terms[q] = (scale[0, 0] * branch[q // per_half, :, low:low + quarter]).astype(jnp.bfloat16)
-
-    def plane_copies(phase, src, dst):
+            leaving[target, :, packed(j, part)] = value.astype(jnp.bfloat16)
+        sum_copy(j, way, target).start()
+
+    def pushes(j, first, last):
+        def step(tau, carry):
+            @pl.when(tau >= z)
+            def _():
+                push(j, 0, line - 1 - tau + z, has_below)
+
+            @pl.when(tau >= line - 1 - z)
+            def _():
+                push(j, 1, tau - (line - 1 - z), has_above)
+
+            return carry
+
+        lax.fori_loop(min(first, line - 1), min(last, line - 1), step, 0)
+
+    def res_copy(j, owner):
+        return remote(
+            res_out.at[:, packed(j)], branch.at[owner, :, packed(j)],
+            core_send.at[2 + j], core_recv.at[2 + j], sibling,
+        )
+
+    def own_sum(j):
+        @pl.when(has_below)
+        def _():
+            sum_copy(j, 0, z).wait_recv()
+
+        @pl.when(has_above)
+        def _():
+            sum_copy(j, 1, z).wait_recv()
+
+        def own(which, part):
+            span = pl.ds(pl.multiple_of(which * rows, rows), rows)
+            value = product(z * both + which * rows, rows, j, part)
+            up = arrived[0, z, span, packed(j, part)].astype(jnp.float32)
+            down = arrived[1, z, span, packed(j, part)].astype(jnp.float32)
+            return value + jnp.where(has_below, up, 0.0) + jnp.where(has_above, down, 0.0)
+
+        for part in range(per_half):
+            res_out[:, packed(j, part)] = own(1 - core, part)
+        res_copy(j, core).start()
+        for part in range(per_half):
+            branch[core, :, packed(j, part)] = own(core, part)
+
+    def plane_copies(j, phase, src, dst, which=range(1, sections)):
         return [
             remote(src(lax.rem(section + d, sections)), dst(d),
-                   plane_send.at[phase, d - 1], plane_recv.at[phase, d - 1], plane[d - 1])
-            for d in range(1, sections)
+                   plane_send.at[j, phase, d - 1], plane_recv.at[j, phase, d - 1], plane[d - 1])
+            for d in which
         ]
 
-    sends = plane_copies(0, lambda to: terms.at[to], lambda d: parts.at[d - 1])
-    for copy in sends:
-        copy.start()
-    source = source_of(flags, context, latent[...], pending[...], section)
-    for h in range(2):
-        columns = slice(h * half, (h + 1) * half)
-        block_out[:, columns] = (source[:, columns] + branch[h]).astype(jnp.bfloat16)
-    total = terms[section].astype(jnp.float32)
-    for d in range(1, sections):
-        sends[d - 1].wait()
-        total = total + parts[d - 1].astype(jnp.float32)
-    grad = total.astype(jnp.bfloat16)
-    lines[z, core] = grad
-    grads[section] = grad
-
-    def line_copy(way, block):
+    def term_copies(j):
+        return plane_copies(
+            j, 0, lambda to: terms.at[to, :, lanes(j)], lambda d: parts.at[d - 1, :, lanes(j)]
+        )
+
+    def share(j):
+        res_copy(j, core).wait_send()
+        res_copy(j, 1 - core).wait_recv()
+        for q in range(sections):
+            value = branch[q // per_half, :, packed(j, q % per_half)]
+            terms[q, :, lanes(j)] = (scale[0, 0] * value).astype(jnp.bfloat16)
+        for copy in term_copies(j):
+            copy.start()
+        for q in range(sections):
+            columns = slice(q * quarter + edges[j], q * quarter + edges[j + 1])
+            source = source_of(
+                flags, context[:, columns], latent[:, columns], pending[:, columns], section
+            )
+            value = branch[q // per_half, :, packed(j, q % per_half)]
+            block_out[:, columns] = (source + value).astype(jnp.bfloat16)
+
+    def line_copy(j, way, block):
+        slot = lines.at[block, core, :, lanes(j)]
         return remote(
-            lines.at[block, core], lines.at[block, core],
-            line_send.at[way, block], line_recv.at[way, block], above if way == 0 else below,
+            slot, slot, line_send.at[j, way, block], line_recv.at[j, way, block],
+            above if way == 0 else below,
         )
 
-    def sib_copy(block):
-        return remote(
-            lines.at[block, core], lines.at[block, core],
-            sib_send.at[block], sib_recv.at[block], sibling,
-        )
-
-    @pl.when(has_above)
-    def _():
-        line_copy(0, z).start()
-
-    @pl.when(has_below)
-    def _():
-        line_copy(1, z).start()
-
-    sib_copy(z).start()
-
-    def gather(phase, buffer):
-        copies = plane_copies(phase, lambda to: buffer.at[section], lambda d: buffer.at[section])
-        for copy in copies:
+    def sib_copy(j, block, owner):
+        slot = lines.at[block, owner, :, lanes(j)]
+        return remote(slot, slot, sib_send.at[j, block], sib_recv.at[j, block], sibling)
+
+    def gather(j, phase, buffer, owner, which=range(1, sections)):
+        slot = buffer.at[owner, :, lanes(j)]
+        return plane_copies(j, phase, lambda to: slot, lambda d: slot, which)
+
+    def gathered(j, phase, buffer):
+        for d in range(1, sections):
+            gather(j, phase, buffer, section, [d])[0].wait_send()
+            sender = lax.rem(section + sections - d, sections)
+            gather(j, phase, buffer, sender, [d])[0].wait_recv()
+
+    def add_up(j):
+        total = terms[section, :, lanes(j)].astype(jnp.float32)
+        copies = term_copies(j)
+        for d in range(1, sections):
+            copies[d - 1].wait()
+            total = total + parts[d - 1, :, lanes(j)].astype(jnp.float32)
+        grad = total.astype(jnp.bfloat16)
+        lines[z, core, :, lanes(j)] = grad
+        grads[section, :, lanes(j)] = grad
+
+        @pl.when(has_above)
+        def _():
+            line_copy(j, 0, z).start()
+
+        @pl.when(has_below)
+        def _():
+            line_copy(j, 1, z).start()
+
+        sib_copy(j, z, core).start()
+        for copy in gather(j, 1, grads, section):
             copy.start()
-        return copies
-
-    def gathered(phase, buffer, copies):
-        for d in range(1, sections):
-            copies[d - 1].wait_send()
-            slot = buffer.at[lax.rem(section + sections - d, sections)]
-            remote(slot, slot, plane_send.at[phase, d - 1], plane_recv.at[phase, d - 1],
-                   plane[d - 1]).wait_recv()
-
-    copies = gather(1, grads)
-    for k in range(1, line):
-        @pl.when(z >= k)
-        def _(k=k):
-            line_copy(0, z - k).wait_recv()
-
-            @pl.when(has_above)
+
+    def spread(j):
+        def step(k, carry):
+            @pl.when(z >= k)
             def _():
-                line_copy(0, z - k).start()
-
-            sib_copy(z - k).start()
-
-        @pl.when(z + k < line)
-        def _(k=k):
-            line_copy(1, z + k).wait_recv()
-
-            @pl.when(has_below)
+                line_copy(j, 0, z - k).wait_recv()
+
+                @pl.when(has_above)
+                def _():
+                    line_copy(j, 0, z - k).start()
+
+                sib_copy(j, z - k, core).start()
+
+            @pl.when(z + k < line)
             def _():
-                line_copy(1, z + k).start()
-
-            sib_copy(z + k).start()
-
-    def sib_wait(block, carry):
-        slot = lines.at[block, 1 - core]
-        sib_copy(block).wait_send()
-        remote(slot, slot, sib_send.at[block], sib_recv.at[block], sibling).wait_recv()
-        return carry
-
-    lax.fori_loop(0, line, sib_wait, 0)
-    everything = lines[...].reshape(line * both, quarter)
-    local = jnp.dot(stored[...], everything, preferred_element_type=jnp.float32)
-    if finish:
-        finals[section] = local.astype(jnp.bfloat16)
-        last = gather(2, finals)
-    else:
-        grad_out[...] = local
-    gathered(1, grads, copies)
-    for q in range(sections):
-        dmd[:, q * quarter:(q + 1) * quarter] = grads[q].astype(jnp.float32)
+                line_copy(j, 1, z + k).wait_recv()
+
+                @pl.when(has_below)
+                def _():
+                    line_copy(j, 1, z + k).start()
+
+                sib_copy(j, z + k, core).start()
+
+            return carry
+
+        lax.fori_loop(1, line, step, 0)
+
+    def project(j):
+        def sib_wait(block, carry):
+            sib_copy(j, block, core).wait_send()
+            sib_copy(j, block, 1 - core).wait_recv()
+            return carry
+
+        lax.fori_loop(0, line, sib_wait, 0)
+        everything = lines[:, :, :, lanes(j)].reshape(line * both, widths[j])
+        local = jnp.dot(stored[...], everything, preferred_element_type=jnp.float32)
+        if finish:
+            finals[section, :, lanes(j)] = local.astype(jnp.bfloat16)
+            for copy in gather(j, 2, finals, section):
+                copy.start()
+        else:
+            grad_out[:, lanes(j)] = local
+
+    pushes(0, 0, line)
+    for j in range(chunks):
+        if j + 1 < chunks:
+            pushes(j + 1, 0, 1)
+        own_sum(j)
+        if j + 1 < chunks:
+            pushes(j + 1, 1, 2)
+        share(j)
+        if j >= 1:
+            spread(j - 1)
+        if j + 1 < chunks:
+            pushes(j + 1, 2, line)
+        add_up(j)
+        if j >= 1:
+            project(j - 1)
+    spread(chunks - 1)
+    project(chunks - 1)
+
+    for j in range(chunks):
+        gathered(j, 1, grads)
+        for q in range(sections):
+            columns = slice(q * quarter + edges[j], q * quarter + edges[j + 1])
+            dmd[:, columns] = grads[q, :, lanes(j)].astype(jnp.float32)
 
     def line_drain(block, carry):
-        @pl.when(jnp.logical_and(block <= z, has_above))
-        def _():
-            line_copy(0, block).wait_send()
-
-        @pl.when(jnp.logical_and(block >= z, has_below))
-        def _():
-            line_copy(1, block).wait_send()
-
-        @pl.when(block > z)
-        def _():
-            sum_copy(0, block).wait_send()
-
-        @pl.when(block < z)
-        def _():
-            sum_copy(1, block).wait_send()
+        for j in range(chunks):
+            @pl.when(jnp.logical_and(block <= z, has_above))
+            def _(j=j):
+                line_copy(j, 0, block).wait_send()
+
+            @pl.when(jnp.logical_and(block >= z, has_below))
+            def _(j=j):
+                line_copy(j, 1, block).wait_send()
+
+            @pl.when(block > z)
+            def _(j=j):
+                sum_copy(j, 0, block).wait_send()
+
+            @pl.when(block < z)
+            def _(j=j):
+                sum_copy(j, 1, block).wait_send()
 
         return carry
 
     lax.fori_loop(0, line, line_drain, 0)
     if finish:
-        gathered(2, finals, last)
-        for q in range(sections):
-            grad_out[:, q * quarter:(q + 1) * quarter] = finals[q].astype(jnp.float32)
+        for j in range(chunks):
+            gathered(j, 2, finals)
+            for q in range(sections):
+                columns = slice(q * quarter + edges[j], q * quarter + edges[j + 1])
+                grad_out[:, columns] = finals[q, :, lanes(j)].astype(jnp.float32)
 
 
 def tail(scale, flags, attn, w_proj, latent, pending, context, stored, finish):
@@ -563,11 +615,11 @@
             pltpu.VMEM((sections, rows, quarter), bf),
             pltpu.VMEM((line, 2, rows, quarter), bf),
             pltpu.VMEM((sections, inner, quarter), bf),
-            dma((3,)), dma((3,)),
-            dma((2, line)), dma((2, line)),
-            dma((3, sections - 1)), dma((3, sections - 1)),
-            dma((2, line)), dma((2, line)),
-            dma((line,)), dma((line,)),
+            dma((5,)), dma((5,)),
+            dma((3, 2, line)), dma((3, 2, line)),
+            dma((3, 3, sections - 1)), dma((3, 3, sections - 1)),
+            dma((3, 2, line)), dma((3, 2, line)),
+            dma((3, line)), dma((3, line)),
         ],
         compiler_params=pltpu.CompilerParams(
             collective_id=1, has_side_effects=True, vmem_limit_bytes=56 << 20

time: 227 us -> 209 us (0.921)
  Pallas kernels: 202 us -> 184 us
    pallas_call x1, Pallas kernels: 135 us -> 117 us  [tail(): pl.pallas_call(functools.partial(tail_kernel, sections, line, finish), ou...]
where the time goes in v4:
time: 209 us
  Pallas kernels  184 us (88%)
  local copies, waits for them, and re-layouts  16.8 us (8%)
  other arithmetic  5.14 us (2%)
  between operations  3.36 us (2%)
    pallas_call x1, Pallas kernels, tail(): pl.pallas_call(functools.partial(tail_kernel, sections, line, finish), ou...  117 us
    pallas_call x1, Pallas kernels, head(): pl.pallas_call(functools.partial(head_kernel, sections, line), out_shape=...  59.1 us
    unnamed x21, local copies, waits for them, and re-layouts  9.45 us
    pallas_call x1, Pallas kernels, attend(): pl.pallas_call(attend_kernel, out_shape=jax.ShapeDtypeStruct((length, hea...  7.94 us
    squeeze x1, local copies, waits for them, and re-layouts, per_device(): w_in = lax.dynamic_index_in_dim(w_qkv, model_index, 0, keepdims=False)  4.24 us

profile of v4, /device:TPU:0, one launch (start us, length us, event | category | flops | bytes accessed | tf_op | source)
XLA Modules:
  0.0 208.9 jit_solution(10209173883455983313)
XLA Ops:
  0.6 1.3 fusion.2
  1.9 1.9 fusion.1
  5.8 0.0 copy-start.6
  5.8 4.2 %dynamic-slice_bitcast_fusion.w_in = bf16[2560,768]{1,0:T(8,128)(2,1)} fusion(bf16[3,2560,768]{2,1,0:T(8,128)(2,1)} %param.15, s32[]{:T(128)S(6)} %select_n.53), kind=kLoop, calls=%fused_computation | loop fusion | bytes 7864324 | tf_op jit(solution)/shard_map/jit(dynamic_index_in_dim)/squeeze | solution.py:640
  10.1 0.0 copy-done.6
  10.1 0.6 add_convert_fusion.flags
  10.7 0.0 copy-start.5
  10.7 59.1 %shard_map.121.qkv = bf16[1536,768]{1,0:T(8,128)(2,1)} custom-call(f32[2,4]{1,0:T(2,128)} %add_convert_fusion.flags, bf16[192,2560]{1,0:T(8,128)(2,1)} %bitcast.25, bf16[192,2560]{1,0:T(8,128)(2,1)} %bitcast.27, f32[1,2560]{1,0:T(1,128)} %context.3, bf16[2560,768]{1,0:T(8,128)(2,1)} %dynamic-slice_bitcast_fusion.w_in), custom_call_target="tpu_custom_call" | custom-call | flops 6039797760 | bytes 16777216 | tf_op jit(solution)/shard_map/pallas_call | solution.py:277
  70.4 0.0 copy-done.5
  70.5 0.3 copy.14.ids_col
  70.8 0.0 copy-start.1
  70.8 1.7 copy-done.1
  72.4 7.9 %shard_map.122.attn = bf16[1536,256]{1,0:T(8,128)(2,1)S(1)} custom-call(s32[1536,1]{1,0:T(8,128)S(1)} %copy.14.ids_col, s32[1,1536]{1,0:T(1,128)S(1)} %fusion.3.ids_row, bf16[1536,768]{1,0:T(8,128)(2,1)S(1)} %copy-done.1), custom_call_target="tpu_custom_call" | custom-call | flops 2415919104 | bytes 3538944 | tf_op jit(solution)/shard_map/pallas_call | solution.py:52
  80.4 0.0 copy-start
  80.4 0.9 copy-done
  81.3 1.4 constant_dynamic-slice_fusion
  82.7 0.0 copy-start.7
  82.7 0.0 copy-start.4
  82.7 0.6 copy.18
  83.3 1.4 copy.16
  84.8 0.0 copy-done.7
  84.8 1.3 fusion
  86.1 0.0 copy-done.4
  86.1 1.2 copy.17
  87.2 116.5 %shard_map.123 = (bf16[192,2560]{1,0:T(8,128)(2,1)}, f32[192,2560]{1,0:T(8,128)}, f32[256,2560]{1,0:T(8,128)}) custom-call(f32[1,1]{1,0:T(1,128)} %bitcast.scale, f32[2,4]{1,0:T(2,128)} %add_convert_fusion.flags, bf16[1536,256]{1,0:T(8,128)(2,1)} %copy-done, bf16[2,256,1280]{2,1,0:T(8,128)(2,1)} %bitcast.22, bf16[192,2560]{1,0:T(8,128)(2,1)} %bitcast.26, ...), custom_call_target="tpu_custom_call" | custom-call | flops 2013265920 | bytes 8388608 | tf_op jit(solution)/shard_map/pallas_call | solution.py:597
  203.7 0.0 copy-start.3
  203.8 0.0 copy-start.2
  203.8 2.4 %copy.22 = bf16[1,1,192,2560]{3,2,1,0:T(8,128)(2,1)} copy(bf16[1,1,192,2560]{3,2,1,0:T(8,128)(2,1)} %bitcast.23) | data formatting | bytes 1966080
  206.1 0.0 copy-done.3
  206.1 1.3 copy.23
  207.4 0.0 copy-done.2
  207.4 1.5 copy.24
  (3 shorter events, 0.0 us)
Async XLA Ops:
  5.8 4.3 %copy-start.6 = (s32[4]{0:T(128)S(1)}, s32[4]{0:T(128)}, u32[]{:S(2)}) copy-start(s32[4]{0:T(128)} %param.10) | copy-start | bytes 52
  10.7 59.8 %copy-start.5 = (s32[2,1,1536]{2,1,0:T(1,128)S(1)}, s32[2,1,1536]{2,1,0:T(1,128)}, u32[]{:S(2)}) copy-start(s32[2,1,1536]{2,1,0:T(1,128)} %param.11) | copy-start | bytes 36868
  70.8 1.7 copy-start.1
  80.4 0.9 copy-start
  82.7 2.1 %copy-start.7 = (f32[4]{0:T(128)S(1)}, f32[4]{0:T(128)}, u32[]{:S(2)}) copy-start(f32[4]{0:T(128)} %constant.26.clone) | copy-start | bytes 52
  82.7 3.4 %copy-start.4 = (bf16[1,1536,256]{2,1,0:T(8,128)(2,1)S(1)}, bf16[1,1536,256]{2,1,0:T(8,128)(2,1)}, u32[]{:S(2)}) copy-start(bf16[1,1536,256]{2,1,0:T(8,128)(2,1)} %param.17) | copy-start | bytes 2359300
  203.7 2.4 %copy-start.3 = (f32[192,2560]{1,0:T(8,128)S(1)}, f32[192,2560]{1,0:T(8,128)}, u32[]{:S(2)}) copy-start(f32[192,2560]{1,0:T(8,128)} %get-tuple-element.7) | copy-start | bytes 5898244
  203.8 3.6 %copy-start.2 = (f32[256,2560]{1,0:T(8,128)S(1)}, f32[256,2560]{1,0:T(8,128)}, u32[]{:S(2)}) copy-start(f32[256,2560]{1,0:T(8,128)} %get-tuple-element.16) | copy-start | bytes 7864324

commit v5 on v4

--- a/solution.py
+++ b/solution.py
@@ -97,9 +97,9 @@
 
 def head_kernel(
     sections, line,
-    flags, latent, pending, context, w_in, qkv,
-    inbox, full, outbox,
-    z_send, z_recv, plane_send, plane_recv, sib_send, sib_recv, slab_send, slab_recv,
+    flags, latent, pending, context, w_qkv, w_out, qkv, w_proj,
+    inbox, full, outbox, w_all, o_all, w_in,
+    z_send, z_recv, plane_send, plane_recv, sib_send, sib_recv, slab_send, slab_recv, load,
 ):
     section = lax.axis_index("section")
     me = lax.axis_index("seq")
@@ -112,6 +112,12 @@
     greet([(None, sibling), (has_above, above), (has_below, below)] + [(None, p) for p in plane])
 
     pieces, chunk = inbox.shape[1], inbox.shape[3]
+    loads = [
+        pltpu.make_async_copy(w_qkv, w_all, load.at[0]),
+        pltpu.make_async_copy(w_out, o_all, load.at[1]),
+    ]
+    for copy in loads:
+        copy.start()
 
     def z_copy(way, block, h):
         return remote(
@@ -149,6 +155,18 @@
         return remote(full.at[z, owner], full.at[z, owner], slab_send, slab_recv, sibling)
 
     slab_copy(core).start()
+
+    for copy, every, chosen in zip(loads, (w_all, o_all), (w_in, w_proj)):
+        copy.wait()
+        amount = min(128, chosen.shape[0])
+
+        def choose(index, carry, every=every, chosen=chosen, amount=amount):
+            rows = pl.ds(pl.multiple_of(index * amount, amount), amount)
+            last = jnp.where(flags[2, 1] > 0.5, every[1, rows, :], every[2, rows, :])
+            chosen[rows, :] = jnp.where(flags[2, 0] > 0.5, every[0, rows, :], last)
+            return carry
+
+        lax.fori_loop(0, chosen.shape[0] // amount, choose, 0)
 
     def plane_copy(d, block, h, owner):
         return remote(
@@ -264,7 +282,7 @@
     lax.fori_loop(0, line * pieces, drain, 0)
 
 
-def head(flags, latent, pending, context, w_in):
+def head(flags, latent, pending, context, w_qkv, w_out):
     sections, seq = lax.axis_size("section"), lax.axis_size("seq")
     line = seq // 2
     rows, width = latent.shape
@@ -276,25 +294,31 @@
     bf = jnp.bfloat16
     return pl.pallas_call(
         functools.partial(head_kernel, sections, line),
-        out_shape=jax.ShapeDtypeStruct((seq * rows, w_in.shape[1]), bf),
-        in_specs=[smem] + [vmem] * 4,
-        out_specs=vmem,
+        out_shape=(
+            jax.ShapeDtypeStruct((seq * rows, w_qkv.shape[2]), bf),
+            jax.ShapeDtypeStruct(w_out.shape[1:], bf),
+        ),
+        in_specs=[smem] + [vmem] * 3 + [pl.BlockSpec(memory_space=pl.ANY)] * 2,
+        out_specs=(vmem, vmem),
         scratch_shapes=[
             pltpu.VMEM((line, pieces, 2, chunk, width), bf),
             pltpu.VMEM((line, 2, sections, pieces, chunk, width), bf),
             pltpu.VMEM((sections - 1, line, pieces, chunk, width), bf),
+            pltpu.VMEM(w_qkv.shape, bf),
+            pltpu.VMEM(w_out.shape, bf),
+            pltpu.VMEM(w_qkv.shape[1:], bf),
             dma((2, line, pieces)), dma((line, pieces)),
             dma((sections - 1, line, pieces)), dma((sections - 1, line, pieces)),
             dma((line, sections, pieces)), dma((line, sections, pieces)),
-            dma(()), dma(()),
+            dma(()), dma(()), dma((2,)),
         ],
         compiler_params=pltpu.CompilerParams(
             collective_id=2, has_side_effects=True, vmem_limit_bytes=56 << 20
         ),
         cost_estimate=pl.CostEstimate(
-            flops=2 * seq * rows * w_in.size, bytes_accessed=16 << 20, transcendentals=0
+            flops=2 * seq * rows * w_qkv.size // w_qkv.shape[0], bytes_accessed=16 << 20, transcendentals=0
         ),
-    )(flags, latent, pending, context, w_in)
+    )(flags, latent, pending, context, w_qkv, w_out)
 
 
 def source_of(flags, context, latent_rows, pending_rows, to):
@@ -307,7 +331,7 @@
     sections, line, finish,
     scale, flags, attn, w2, latent, pending, context, stored,
     block_out, dmd, grad_out,
-    attn_sib, w_sib, arrived, leaving, res_out, branch, terms, parts, grads, lines, finals,
+    attn_sib, w_sib, arrived, leaving, res_out, branch, terms, parts, grads, lines, finals, stored_t,
     core_send, core_recv, sum_send, sum_recv, plane_send, plane_recv,
     line_send, line_recv, sib_send, sib_recv,
 ):
@@ -323,7 +347,7 @@
 
     rows = latent.shape[0]
     both = 2 * rows
-    half = w2.shape[2]
+    half = w2.shape[1] // 2
     quarter = terms.shape[2]
     per_half = half // quarter
     tiles = quarter // 128
@@ -340,7 +364,9 @@
         first = per_half * edges[j] + part * widths[j]
         return slice(first, first + widths[j])
 
-    w_copy = remote(w2.at[1 - core], w_sib, core_send.at[0], core_recv.at[0], sibling)
+    w_copy = remote(
+        w2.at[:, pl.ds(pl.multiple_of((1 - core) * half, 128), half)], w_sib,
+        core_send.at[0], core_recv.at[0], sibling)
     a_copy = remote(attn, attn_sib, core_send.at[1], core_recv.at[1], sibling)
     w_copy.start()
     a_copy.start()
@@ -350,8 +376,9 @@
     def product(first, amount, j, part):
         span = pl.ds(pl.multiple_of(first, rows), amount)
         columns = slice(part * quarter + edges[j], part * quarter + edges[j + 1])
+        mine = pl.ds(pl.multiple_of(core * half + columns.start, 128), widths[j])
         return jnp.dot(
-            attn[span, :], w2[core, :, columns], preferred_element_type=jnp.float32
+            attn[span, :], w2[:, mine], preferred_element_type=jnp.float32
         ) + jnp.dot(
             attn_sib[span, :], w_sib[:, columns], preferred_element_type=jnp.float32
         )
@@ -522,7 +549,7 @@
 
         lax.fori_loop(0, line, sib_wait, 0)
         everything = lines[:, :, :, lanes(j)].reshape(line * both, widths[j])
-        local = jnp.dot(stored[...], everything, preferred_element_type=jnp.float32)
+        local = jnp.dot(stored_t[...], everything, preferred_element_type=jnp.float32)
         if finish:
             finals[section, :, lanes(j)] = local.astype(jnp.bfloat16)
             for copy in gather(j, 2, finals, section):
@@ -531,6 +558,7 @@
             grad_out[:, lanes(j)] = local
 
     pushes(0, 0, line)
+    stored_t[...] = stored[...].T
     for j in range(chunks):
         if j + 1 < chunks:
             pushes(j + 1, 0, 1)
@@ -589,7 +617,6 @@
     rows, width = latent.shape
     length, inner = attn.shape
     half, quarter = width // 2, width // sections
-    w2 = w_proj.reshape(inner, 2, half).transpose(1, 0, 2)
     vmem = pl.BlockSpec(memory_space=pltpu.VMEM)
     smem = pl.BlockSpec(memory_space=pltpu.SMEM)
     bf, f32 = jnp.bfloat16, jnp.float32
@@ -615,6 +642,7 @@
             pltpu.VMEM((sections, rows, quarter), bf),
             pltpu.VMEM((line, 2, rows, quarter), bf),
             pltpu.VMEM((sections, inner, quarter), bf),
+            pltpu.VMEM((inner, length), bf),
             dma((5,)), dma((5,)),
             dma((3, 2, line)), dma((3, 2, line)),
             dma((3, 3, sections - 1)), dma((3, 3, sections - 1)),
@@ -627,7 +655,7 @@
         cost_estimate=pl.CostEstimate(
             flops=2 * length * inner * width, bytes_accessed=8 << 20, transcendentals=0
         ),
-    )(scale, flags, attn, w2, latent, pending, context, stored)
+    )(scale, flags, attn, w_proj, latent, pending, context, stored)
 
 
 def per_device(roles, block_ids, latent, pending, context, w_qkv, w_out, stored_attn):
@@ -637,19 +665,17 @@
     section_role = jnp.sum(jnp.where(places == section, roles, 0))
     model_index = jnp.sum(jnp.where(places == section_role, jnp.array([0, 1, 1, 2], jnp.int32), 0))
     score_weight = jnp.sum(jnp.where(places == section_role, weight_table, 0.0))
-    w_in = lax.dynamic_index_in_dim(w_qkv, model_index, 0, keepdims=False)
-    w_proj = lax.dynamic_index_in_dim(w_out, model_index, 0, keepdims=False)
     is_generator = section_role == 0
     flags = jnp.stack(
-        [roles == 0, jnp.logical_or(roles == 1, roles == 3)]
+        [roles == 0, jnp.logical_or(roles == 1, roles == 3), places == model_index]
     ).astype(jnp.float32)
-    qkv_rows = head(flags, latent[0], pending[0], context, w_in)
+    qkv_rows, w_proj = head(flags, latent[0], pending[0], context, w_qkv, w_out)
     frame_ids = jnp.where(is_generator, block_ids[0, 0], block_ids[1, 0])
     attn = attend(qkv_rows, frame_ids)
     finish = lax.axis_size("dp") == 1
     block_out, gradient, grad_out = tail(
         score_weight.reshape(1, 1), flags, attn, w_proj, latent[0], pending[0], context,
-        stored_attn[0].T, finish,
+        stored_attn[0], finish,
     )
     if not finish:
         grad_out = lax.psum(grad_out, "dp").astype(jnp.bfloat16)

time: 209 us -> 201 us (0.962)
  local copies, waits for them, and re-layouts: 16.8 us -> 7.96 us
  other arithmetic: 5.14 us -> 8.47 us
    squeeze x1 -> x0, local copies, waits for them, and re-layouts: 4.24 us -> none  [per_device(): w_in = lax.dynamic_index_in_dim(w_qkv, model_index, 0, keepdims=False)]
    unnamed x21 -> x11, local copies, waits for them, and re-layouts: 9.45 us -> 7.66 us
where the time goes in v5:
time: 201 us
  Pallas kernels  183 us (91%)
  other arithmetic  8.47 us (4%)
  local copies, waits for them, and re-layouts  7.96 us (4%)
    pallas_call x1, Pallas kernels, tail(): pl.pallas_call(functools.partial(tail_kernel, sections, line, finish), ou...  117 us
    pallas_call x1, Pallas kernels, head(): pl.pallas_call(functools.partial(head_kernel, sections, line), out_shape=...  58.8 us
    unnamed x11, local copies, waits for them, and re-layouts  7.66 us
    pallas_call x1, Pallas kernels, attend(): pl.pallas_call(attend_kernel, out_shape=jax.ShapeDtypeStruct((length, hea...  7.63 us

profile of v5, /device:TPU:0, one launch (start us, length us, event | category | flops | bytes accessed | tf_op | source)
XLA Modules:
  0.0 200.8 jit_solution(2739887170210088674)
XLA Ops:
  0.6 1.3 fusion.2
  2.6 1.9 fusion.1
  4.5 0.7 iota_compare_fusion
  5.2 1.9 fusion
  7.1 0.7 compare_bitcast_fusion
  7.7 0.6 add_convert_fusion.flags
  8.3 0.7 fusion.3.ids_row
  9.1 0.7 fusion.4
  9.8 0.3 copy.13.ids_col
  10.1 58.8 %shard_map.121 = (bf16[1536,768]{1,0:T(8,128)(2,1)}, bf16[256,2560]{1,0:T(8,128)(2,1)}) custom-call(f32[3,4]{1,0:T(4,128)} %add_convert_fusion.flags, bf16[192,2560]{1,0:T(8,128)(2,1)} %bitcast.16, bf16[192,2560]{1,0:T(8,128)(2,1)} %bitcast.18, f32[1,2560]{1,0:T(1,128)} %context.3, bf16[3,2560,768]{2,1,0:T(8,128)(2,1)} %w_qkv.1, bf16[3,256,2560]{2,1,0:T(8,128)(2,1)} %w_out.1), custom_call_target="tpu_custom_call" | custom-call | flops 6039797760 | bytes 16777216 | tf_op jit(solution)/shard_map/pallas_call | solution.py:295
  68.9 0.0 copy-start.1
  68.9 1.7 copy-done.1
  70.6 7.6 %shard_map.122.attn = bf16[1536,256]{1,0:T(8,128)(2,1)S(1)} custom-call(s32[1536,1]{1,0:T(8,128)S(1)} %copy.13.ids_col, s32[1,1536]{1,0:T(1,128)S(1)} %fusion.3.ids_row, bf16[1536,768]{1,0:T(8,128)(2,1)S(1)} %copy-done.1), custom_call_target="tpu_custom_call" | custom-call | flops 2415919104 | bytes 3538944 | tf_op jit(solution)/shard_map/pallas_call | solution.py:52
  78.2 0.0 copy-start
  78.2 0.9 copy-done
  79.1 116.6 %shard_map.123 = (bf16[192,2560]{1,0:T(8,128)(2,1)}, f32[192,2560]{1,0:T(8,128)}, f32[256,2560]{1,0:T(8,128)}) custom-call(f32[1,1]{1,0:T(1,128)} %bitcast.scale, f32[3,4]{1,0:T(4,128)} %add_convert_fusion.flags, bf16[1536,256]{1,0:T(8,128)(2,1)} %copy-done, bf16[256,2560]{1,0:T(8,128)(2,1)} %get-tuple-element.9.w2, bf16[192,2560]{1,0:T(8,128)(2,1)} %bitcast.17, ...), custom_call_target="tpu_custom_call" | custom-call | flops 2013265920 | bytes 8388608 | tf_op jit(solution)/shard_map/pallas_call | solution.py:624
  195.7 0.0 copy-start.3
  195.7 0.0 copy-start.2
  195.7 2.4 %copy.17 = bf16[1,1,192,2560]{3,2,1,0:T(8,128)(2,1)} copy(bf16[1,1,192,2560]{3,2,1,0:T(8,128)(2,1)} %bitcast.15) | data formatting | bytes 1966080
  198.1 0.0 copy-done.3
  198.1 1.3 copy.18
  199.3 0.0 copy-done.2
  199.3 1.5 copy.19
Async XLA Ops:
  68.9 1.7 copy-start.1
  78.2 0.9 copy-start
  195.7 2.4 %copy-start.3 = (f32[192,2560]{1,0:T(8,128)S(1)}, f32[192,2560]{1,0:T(8,128)}, u32[]{:S(2)}) copy-start(f32[192,2560]{1,0:T(8,128)} %get-tuple-element.11) | copy-start | bytes 5898244
  195.7 3.6 %copy-start.2 = (f32[256,2560]{1,0:T(8,128)S(1)}, f32[256,2560]{1,0:T(8,128)}, u32[]{:S(2)}) copy-start(f32[256,2560]{1,0:T(8,128)} %get-tuple-element.20) | copy-start | bytes 7864324

commit v6 on v5

--- a/solution.py
+++ b/solution.py
@@ -580,7 +580,7 @@
         gathered(j, 1, grads)
         for q in range(sections):
             columns = slice(q * quarter + edges[j], q * quarter + edges[j + 1])
-            dmd[:, columns] = grads[q, :, lanes(j)].astype(jnp.float32)
+            dmd[:, columns] = grads[q, :, lanes(j)]
 
     def line_drain(block, carry):
         for j in range(chunks):
@@ -608,7 +608,7 @@
             gathered(j, 2, finals)
             for q in range(sections):
                 columns = slice(q * quarter + edges[j], q * quarter + edges[j + 1])
-                grad_out[:, columns] = finals[q, :, lanes(j)].astype(jnp.float32)
+                grad_out[:, columns] = finals[q, :, lanes(j)]
 
 
 def tail(scale, flags, attn, w_proj, latent, pending, context, stored, finish):
@@ -625,8 +625,8 @@
         functools.partial(tail_kernel, sections, line, finish),
         out_shape=(
             jax.ShapeDtypeStruct((rows, width), bf),
-            jax.ShapeDtypeStruct((rows, width), f32),
-            jax.ShapeDtypeStruct((inner, width if finish else quarter), f32),
+            jax.ShapeDtypeStruct((rows, width), bf),
+            jax.ShapeDtypeStruct((inner, width if finish else quarter), bf if finish else f32),
         ),
         in_specs=[smem] * 2 + [vmem] * 6,
         out_specs=(vmem,) * 3,
@@ -679,8 +679,10 @@
     )
     if not finish:
         grad_out = lax.psum(grad_out, "dp").astype(jnp.bfloat16)
-        grad_out = lax.all_gather(grad_out, "section", axis=1, tiled=True).astype(jnp.float32)
-    return (block_out[None, None], gradient[None], grad_out)
+        grad_out = lax.all_gather(grad_out, "section", axis=1, tiled=True)
+    return (
+        block_out[None, None], gradient[None].astype(jnp.float32), grad_out.astype(jnp.float32)
+    )
 
 
 def solution(mesh):

time: 201 us -> 199 us (0.990)
  local copies, waits for them, and re-layouts: 7.96 us -> 3.78 us
  other arithmetic: 8.47 us -> 11.1 us
    convert_element_type x0 -> x2, other arithmetic: none -> 4.69 us  [the longest x1 3.2 us: per_device(): grad_out.astype(jnp.float32)]
    unnamed x11 -> x13, local copies, waits for them, and re-layouts: 7.66 us -> 3.49 us
where the time goes in v6:
time: 199 us
  Pallas kernels  182 us (91%)
  other arithmetic  11.1 us (6%)
  local copies, waits for them, and re-layouts  3.78 us (2%)
    pallas_call x1, Pallas kernels, tail(): pl.pallas_call(functools.partial(tail_kernel, sections, line, finish), ou...  116 us
    pallas_call x1, Pallas kernels, head(): pl.pallas_call(functools.partial(head_kernel, sections, line), out_shape=...  58.8 us
    pallas_call x1, Pallas kernels, attend(): pl.pallas_call(attend_kernel, out_shape=jax.ShapeDtypeStruct((length, hea...  7.6 us

profile of v6, /device:TPU:0, one launch (start us, length us, event | category | flops | bytes accessed | tf_op | source)
XLA Modules:
  0.0 198.7 jit_solution(17383036461129071988)
XLA Ops:
  0.6 1.3 fusion.2
  1.9 1.9 fusion.1
  3.9 0.7 iota_compare_fusion
  4.5 0.7 compare_bitcast_fusion
  5.2 0.6 add_convert_fusion.flags
  5.8 0.0 copy-start.4
  5.8 58.8 %shard_map.121 = (bf16[1536,768]{1,0:T(8,128)(2,1)}, bf16[256,2560]{1,0:T(8,128)(2,1)}) custom-call(f32[3,4]{1,0:T(4,128)} %add_convert_fusion.flags, bf16[192,2560]{1,0:T(8,128)(2,1)} %bitcast.17, bf16[192,2560]{1,0:T(8,128)(2,1)} %bitcast.19, f32[1,2560]{1,0:T(1,128)} %context.3, bf16[3,2560,768]{2,1,0:T(8,128)(2,1)} %w_qkv.1, bf16[3,256,2560]{2,1,0:T(8,128)(2,1)} %w_out.1), custom_call_target="tpu_custom_call" | custom-call | flops 6039797760 | bytes 16777216 | tf_op jit(solution)/shard_map/pallas_call | solution.py:295
  65.3 0.0 copy-done.4
  65.3 0.3 copy.13.ids_col
  65.6 0.0 copy-start.1
  65.6 1.7 copy-done.1
  67.3 0.0 copy-start.5
  67.3 7.6 %shard_map.122.attn = bf16[1536,256]{1,0:T(8,128)(2,1)S(1)} custom-call(s32[1536,1]{1,0:T(8,128)S(1)} %copy.13.ids_col, s32[1,1536]{1,0:T(1,128)S(1)} %fusion.3.ids_row, bf16[1536,768]{1,0:T(8,128)(2,1)S(1)} %copy-done.1), custom_call_target="tpu_custom_call" | custom-call | flops 2415919104 | bytes 3538944 | tf_op jit(solution)/shard_map/pallas_call | solution.py:52
  74.9 0.0 copy-start
  74.9 0.9 copy-done
  75.8 0.0 copy-done.5
  75.8 1.3 fusion
  77.1 115.9 %shard_map.123 = (bf16[192,2560]{1,0:T(8,128)(2,1)}, bf16[192,2560]{1,0:T(8,128)(2,1)}, bf16[256,2560]{1,0:T(8,128)(2,1)}) custom-call(f32[1,1]{1,0:T(1,128)} %bitcast.scale, f32[3,4]{1,0:T(4,128)} %add_convert_fusion.flags, bf16[1536,256]{1,0:T(8,128)(2,1)} %copy-done, bf16[256,2560]{1,0:T(8,128)(2,1)} %get-tuple-element.9.w2, bf16[192,2560]{1,0:T(8,128)(2,1)} %bitcast.18, ...), custom_call_target="tpu_custom_call" | custom-call | flops 2013265920 | bytes 8388608 | tf_op jit(solution)/shard_map/pallas_call | solution.py:624
  193.0 0.0 copy-start.3
  193.0 3.2 %convert_element_type.15 = f32[256,2560]{1,0:T(8,128)} convert(bf16[256,2560]{1,0:T(8,128)(2,1)} %get-tuple-element.12) | non-fusion elementwise | flops 655360 | bytes 3932160 | tf_op jit(solution)/shard_map/convert_element_type | solution.py:684
  196.2 0.0 copy-start.2
  196.2 0.0 copy-done.3
  196.2 1.5 bitcast_convert_fusion
  197.7 0.0 copy-done.2
  197.7 0.9 copy.15
  (2 shorter events, 0.0 us)
Async XLA Ops:
  5.8 59.5 %copy-start.4 = (s32[2,1,1536]{2,1,0:T(1,128)S(1)}, s32[2,1,1536]{2,1,0:T(1,128)}, u32[]{:S(2)}) copy-start(s32[2,1,1536]{2,1,0:T(1,128)} %param.11) | copy-start | bytes 36868
  65.6 1.7 copy-start.1
  67.3 8.5 %copy-start.5 = (f32[4]{0:T(128)S(1)}, f32[4]{0:T(128)}, u32[]{:S(2)}) copy-start(f32[4]{0:T(128)} %constant.18.clone) | copy-start | bytes 52
  74.9 0.9 copy-start
  193.0 3.2 %copy-start.3 = (bf16[192,2560]{1,0:T(8,128)(2,1)S(1)}, bf16[192,2560]{1,0:T(8,128)(2,1)}, u32[]{:S(2)}) copy-start(bf16[192,2560]{1,0:T(8,128)(2,1)} %get-tuple-element.11) | copy-start | bytes 2949124
  196.2 1.5 copy-start.2
